TPU v7x, 1024 devices: a whole 8x8x8 slice. The times are simulated.
1024 devices in a mesh: xi: 64 (over y_lo, z, core), eta: 16 (over y_hi, x).
Axes of the slice: x: 8, y: 8 (y_hi: 2, y_lo: 4; y = y_hi * 4 + y_lo), z: 8, core: 2. Of those that a mesh axis runs over, the one named last changes fastest.
Arguments:
- mantle_disp: float32 [3, 272, 17280], P(None, 'eta', 'xi'), may hold values from -6 to 6
- mantle_vel: float32 [3, 272, 17280], P(None, 'eta', 'xi'), may hold values from -6 to 6
- mantle_acc: float32 [3, 272, 17280], P(None, 'eta', 'xi'), may hold values from -12 to 12
- mantle_metric: float32 [3, 272, 17280], P(None, 'eta', 'xi'), may hold values from 0.7 to 1.4
- mantle_moduli: float32 [2, 272, 17280], P(None, 'eta', 'xi'), may hold values from 0.02 to 0.2
- mantle_rho: float32 [272, 17280], P('eta', 'xi'), may hold values from 0.5 to 2
- core_pot: float32 [272, 17280], P('eta', 'xi'), may hold values from -6 to 6
- core_rate: float32 [272, 17280], P('eta', 'xi'), may hold values from -6 to 6
- core_accel: float32 [272, 17280], P('eta', 'xi'), may hold values from -12 to 12
- core_metric: float32 [3, 272, 17280], P(None, 'eta', 'xi'), may hold values from 0.7 to 1.4
- core_kappa: float32 [272, 17280], P('eta', 'xi'), may hold values from 0.02 to 0.2
- core_rho: float32 [272, 17280], P('eta', 'xi'), may hold values from 0.5 to 2
- inner_disp: float32 [3, 272, 9600], P(None, 'eta', 'xi'), may hold values from -6 to 6
- inner_vel: float32 [3, 272, 9600], P(None, 'eta', 'xi'), may hold values from -6 to 6
- inner_acc: float32 [3, 272, 9600], P(None, 'eta', 'xi'), may hold values from -12 to 12
- inner_metric: float32 [3, 272, 9600], P(None, 'eta', 'xi'), may hold values from 0.7 to 1.4
- inner_moduli: float32 [2, 272, 9600], P(None, 'eta', 'xi'), may hold values from 0.02 to 0.2
- inner_rho: float32 [272, 9600], P('eta', 'xi'), may hold values from 0.5 to 2
Outputs:
- mantle_disp_new: float32 [3, 272, 17280], P(None, 'eta', 'xi')
- mantle_vel_new: float32 [3, 272, 17280], P(None, 'eta', 'xi')
- mantle_acc_new: float32 [3, 272, 17280], P(None, 'eta', 'xi')
- core_pot_new: float32 [272, 17280], P('eta', 'xi')
- core_rate_new: float32 [272, 17280], P('eta', 'xi')
- core_accel_new: float32 [272, 17280], P('eta', 'xi')
- inner_disp_new: float32 [3, 272, 9600], P(None, 'eta', 'xi')
- inner_vel_new: float32 [3, 272, 9600], P(None, 'eta', 'xi')
- inner_acc_new: float32 [3, 272, 9600], P(None, 'eta', 'xi')
All inputs are finite; a program needn't handle non-finite values.
Results may differ from a plain program's by a relative error of at most 0.0001.
Values sent between devices are 32-bit elements; how exact they have to be, the bound alone decides.
A program may use at most 64 MiB of HBM per device.

v0:
```python
import math

import jax
import jax.numpy as jnp
import numpy as np
from jax import lax
from jax.sharding import PartitionSpec as P

EX = 1
MANTLE_LAYERS = 2
CORE_LAYERS = 2
INNER_LAYERS = 1


time_step = 0.1
highest = lax.Precision.HIGHEST


def with_halo(cells, sides, width, closed):
    for axis, dim in sides:
        count = lax.axis_size(axis)
        ends = count if closed else count - 1
        head = lax.slice_in_dim(cells, 0, width, axis=dim)
        tail = lax.slice_in_dim(cells, cells.shape[dim] - width, cells.shape[dim], axis=dim)
        cells = jnp.concatenate(
            [
                lax.ppermute(tail, axis, [(i, (i + 1) % count) for i in range(ends)]),
                cells,
                lax.ppermute(head, axis, [((i + 1) % count, i) for i in range(ends)]),
            ],
            axis=dim,
        )
    return cells


def gll_tables():
    radical = math.sqrt(3.0 / 7.0)
    points = np.array([-1.0, -radical, 0.0, radical, 1.0])
    weights = np.array([0.1, 49.0 / 90.0, 32.0 / 45.0, 49.0 / 90.0, 0.1])
    products = np.array(
        [
            np.prod(
                [
                    points[first_node] - points[other_node]
                    for other_node in range(5)
                    if other_node != first_node
                ]
            )
            for first_node in range(5)
        ]
    )
    slopes = np.zeros((5, 5))
    for first_node in range(5):
        for second_node in range(5):
            if first_node == second_node:
                slopes[first_node, second_node] = np.sum(
                    [
                        1.0 / (points[first_node] - points[other_node])
                        for other_node in range(5)
                        if other_node != first_node
                    ]
                )
            else:
                slopes[first_node, second_node] = products[first_node] / (
                    products[second_node] * (points[first_node] - points[second_node])
                )
    return (weights, slopes)


def spread_table(element_count):
    spread = np.zeros((4 * element_count + 1, 5 * element_count))
    for element in range(element_count):
        for node_index in range(5):
            spread[4 * element + node_index, 5 * element + node_index] = 1.0
    return spread


def radial_maps(element_count):
    weights, slopes = gll_tables()
    spread = spread_table(element_count)
    derive = np.kron(np.eye(element_count), slopes.T)
    element_weights = np.tile(weights, element_count)
    lumped = spread @ element_weights
    return (
        jnp.asarray(spread, jnp.float32),
        jnp.asarray(derive, jnp.float32),
        jnp.asarray(element_weights, jnp.float32),
        jnp.asarray(lumped, jnp.float32),
    )


def lateral_maps(count_x):
    weights, slopes = gll_tables()
    spread_x = spread_table(count_x)
    derive_x = np.kron(np.eye(count_x), slopes.T)
    weights_x = np.tile(weights, count_x)
    widen_table = np.kron(np.eye(5), np.kron(spread_x, np.eye(6)))
    along_y = np.kron(slopes.T, np.eye(30 * count_x))
    along_x = np.kron(np.eye(5), np.kron(derive_x, np.eye(6)))
    node_weights = np.kron(weights, np.kron(weights_x, np.ones(6)))
    return (
        jnp.asarray(widen_table, jnp.float32),
        jnp.asarray(along_y, jnp.float32),
        jnp.asarray(along_x, jnp.float32),
        jnp.asarray(node_weights, jnp.float32),
    )


def lumped_lines(count_y, count_x):
    weights = gll_tables()[0]
    lumped_y = spread_table(count_y) @ np.tile(weights, count_y)
    lumped_x = spread_table(count_x) @ np.tile(weights, count_x)
    return (jnp.asarray(lumped_y, jnp.float32), jnp.asarray(lumped_x, jnp.float32))


def to_radial(native, radial):
    shaped = native.reshape(native.shape[:-1] + (native.shape[-1] // radial, radial))
    return jnp.moveaxis(shaped, -1, -3)


def to_blocked(radial_first, across):
    moved = jnp.moveaxis(radial_first, -3, -1)
    return moved.reshape(moved.shape[:-2] + (1, across, 6, moved.shape[-1]))


def to_slab(grid):
    rows_local = grid.shape[-2]
    width = grid.shape[-1]
    count_y = (rows_local - 1) // 4
    main_rows = grid[..., :-1, :].reshape(grid.shape[:-2] + (count_y, 4 * width))
    end_rows = grid[..., 4::4, :]
    return jnp.concatenate([main_rows, end_rows], axis=-1)


def from_slab(slab, width):
    count_y = slab.shape[-2]
    front = slab[..., : 4 * width].reshape(slab.shape[:-2] + (4 * count_y, width))
    zero_row = jnp.zeros(slab.shape[:-2] + (1, width), slab.dtype)
    front = jnp.concatenate([front, zero_row], axis=-2)
    tail = slab[..., 4 * width :]
    padded = jnp.concatenate(
        [jnp.zeros(slab.shape[:-2] + (count_y, 3, width), slab.dtype), tail[..., None, :]], axis=-2
    )
    back = jnp.concatenate(
        [zero_row, padded.reshape(slab.shape[:-2] + (4 * count_y, width))], axis=-2
    )
    return front + back


def widen(grid, lateral, radial):
    slab = jnp.matmul(to_slab(grid), lateral[0], precision=highest)
    return jnp.einsum("...rez,rd->...dez", slab, radial[0], precision=highest)


def narrow(nodes, lateral, radial, width):
    slab = jnp.einsum("...dez,rd->...rez", nodes, radial[0], precision=highest)
    slab = jnp.matmul(slab, lateral[0].T, precision=highest)
    return from_slab(slab, width)


def node_slopes(nodes, lateral, radial):
    along_y = jnp.matmul(nodes, lateral[1], precision=highest)
    along_x = jnp.matmul(nodes, lateral[2], precision=highest)
    along_r = jnp.einsum("...dez,df->...fez", nodes, radial[1], precision=highest)
    return (along_y, along_x, along_r)


def node_adjoint(flux_y, flux_x, flux_r, lateral, radial):
    summed = jnp.matmul(flux_y, lateral[1].T, precision=highest)
    summed = summed + jnp.matmul(flux_x, lateral[2].T, precision=highest)
    summed = summed + jnp.einsum("...fez,df->...dez", flux_r, radial[1], precision=highest)
    return summed


def elastic_slab(displace, metric, moduli, lateral, radial, across):
    radial_count = radial[0].shape[0]
    width = across * 6
    node_values = widen(to_radial(displace, radial_count), lateral, radial)
    inverse_scale = widen(to_radial(metric, radial_count), lateral, radial)
    lame_nodes = widen(to_radial(moduli, radial_count), lateral, radial)
    slope_y, slope_x, slope_r = node_slopes(node_values, lateral, radial)
    physical = jnp.stack(
        [slope_y * inverse_scale[0], slope_x * inverse_scale[1], slope_r * inverse_scale[2]], axis=1
    )
    dilation = physical[0, 0] + physical[1, 1] + physical[2, 2]
    strain = 0.5 * (physical + jnp.swapaxes(physical, 0, 1))
    identity = jnp.eye(3, dtype=node_values.dtype).reshape(3, 3, 1, 1, 1)
    stress = 2.0 * lame_nodes[1] * strain + lame_nodes[0] * dilation * identity
    node_weight = radial[2][:, None, None] * lateral[3][None, None, :]
    volume = node_weight / (inverse_scale[0] * inverse_scale[1] * inverse_scale[2])
    fluxes = stress * (volume * inverse_scale)[None]
    summed = node_adjoint(fluxes[:, 0], fluxes[:, 1], fluxes[:, 2], lateral, radial)
    return to_blocked(-narrow(summed, lateral, radial, width), across)


def fluid_slab(potential, metric, density, lateral, radial, across):
    radial_count = radial[0].shape[0]
    width = across * 6
    node_values = widen(to_radial(potential, radial_count), lateral, radial)
    inverse_scale = widen(to_radial(metric, radial_count), lateral, radial)
    density_nodes = widen(to_radial(density, radial_count), lateral, radial)
    slope_y, slope_x, slope_r = node_slopes(node_values, lateral, radial)
    node_weight = radial[2][:, None, None] * lateral[3][None, None, :]
    volume = node_weight / (inverse_scale[0] * inverse_scale[1] * inverse_scale[2] * density_nodes)
    summed = node_adjoint(
        volume * inverse_scale[0] * inverse_scale[0] * slope_y,
        volume * inverse_scale[1] * inverse_scale[1] * slope_x,
        volume * inverse_scale[2] * inverse_scale[2] * slope_r,
        lateral,
        radial,
    )
    return to_blocked(-narrow(summed, lateral, radial, width), across)


def native_volume(metric, lumped_y, lumped_x, radial):
    line_weights = jnp.kron(lumped_x, jnp.kron(jnp.ones((6,), jnp.float32), radial[3]))
    weight_grid = lumped_y[:, None] * line_weights[None, :]
    return weight_grid / (metric[0] * metric[1] * metric[2])


def pack(stacked):
    channels = stacked.shape[0]
    reordered = jnp.moveaxis(stacked[:, :, 0], 0, 3)
    return reordered.reshape(reordered.shape[:3] + (channels * reordered.shape[-1],))


def unpack(packed, channels, radial):
    shaped = packed.reshape(packed.shape[:3] + (channels, radial))
    return jnp.moveaxis(shaped, 3, 0)[:, :, None]


def place(edge_strip, offset, active, length):
    zero_line = jnp.zeros((length,) + edge_strip.shape[1:], edge_strip.dtype)
    return lax.dynamic_update_slice_in_dim(zero_line, jnp.where(active, edge_strip, 0.0), offset, 0)


def segment(seam_line, offset, extent):
    return lax.dynamic_slice_in_dim(seam_line, offset, extent, 0)


def assemble(packed, move_columns, move_rows, sum_lines):
    xi_index = lax.axis_index("xi")
    xi_count = lax.axis_size("xi")
    eta_index = lax.axis_index("eta")
    eta_count = lax.axis_size("eta")
    rows_local = packed.shape[0]
    across = packed.shape[1]
    length = (across - 1) * xi_count + 1
    beside_all = move_columns(jnp.stack([packed[:, 0], packed[:, -1]]))
    from_left = beside_all[0]
    from_right = beside_all[-1]
    empty_groups = jnp.zeros_like(from_left[:, 0:2])
    left_turned = jnp.concatenate([from_left[:, 3:4], from_left[:, 0:3], empty_groups], axis=1)
    right_turned = jnp.concatenate([from_right[:, 1:4], from_right[:, 0:1], empty_groups], axis=1)
    from_left = jnp.where(xi_index == 0, left_turned, from_left)
    from_right = jnp.where(xi_index == xi_count - 1, right_turned, from_right)
    packed = packed.at[:, 0].add(from_left).at[:, -1].add(from_right)
    beside_all = move_rows(jnp.stack([packed[0], packed[-1]]))
    packed = packed.at[0].add(beside_all[0]).at[-1].add(beside_all[-1])
    on_top = eta_index == eta_count - 1
    on_bottom = eta_index == 0
    on_left = xi_index == 0
    on_right = xi_index == xi_count - 1
    own_x = ((jnp.arange(across) < across - 1) | on_right).astype(packed.dtype)[:, None]
    own_y = ((jnp.arange(rows_local) < rows_local - 1) | on_top).astype(packed.dtype)[:, None]
    start_x = xi_index * (across - 1)
    back_x = (xi_count - 1 - xi_index) * (across - 1)
    start_y = eta_index * (rows_local - 1)
    back_y = (eta_count - 1 - eta_index) * (rows_local - 1)
    row_top = packed[-1]
    row_bottom = packed[0]
    col_left = packed[:, 0]
    col_right = packed[:, -1]
    equator_north = place(row_top[:, 0:4] * own_x[:, :, None], start_x, on_top, length)
    equator_south = place(row_bottom[:, 0:4] * own_x[:, :, None], start_x, on_bottom, length)
    zero_line = jnp.zeros_like(equator_north[:, 0])
    north_row_part = jnp.stack(
        [
            place(row_bottom[:, 4] * own_x, start_x, on_bottom, length),
            zero_line,
            place((row_top[:, 4] * own_x)[::-1], back_x, on_top, length),
            zero_line,
        ],
        axis=1,
    )
    south_row_part = jnp.stack(
        [
            place(row_top[:, 5] * own_x, start_x, on_top, length),
            zero_line,
            place((row_bottom[:, 5] * own_x)[::-1], back_x, on_bottom, length),
            zero_line,
        ],
        axis=1,
    )
    north_column_part = jnp.stack(
        [
            place(col_right[:, 4] * own_y, start_y, on_right, length),
            place((col_left[:, 4] * own_y)[::-1], back_y, on_left, length),
        ],
        axis=1,
    )
    south_column_part = jnp.stack(
        [
            place((col_right[:, 5] * own_y)[::-1], back_y, on_right, length),
            place(col_left[:, 5] * own_y, start_y, on_left, length),
        ],
        axis=1,
    )
    row_table = jnp.stack([equator_north + north_row_part, equator_south + south_row_part])
    column_table = jnp.stack([north_column_part, south_column_part])
    summed_lines = sum_lines(row_table, column_table)
    north_lines = summed_lines[0]
    south_lines = summed_lines[1]
    top_values = jnp.concatenate(
        [
            segment(north_lines, start_x, across),
            segment(north_lines[:, 2], back_x, across)[::-1][:, None],
            segment(south_lines[:, 0], start_x, across)[:, None],
        ],
        axis=1,
    )
    packed = packed.at[-1].set(jnp.where(on_top, top_values, packed[-1]))
    bottom_values = jnp.concatenate(
        [
            segment(south_lines, start_x, across),
            segment(north_lines[:, 0], start_x, across)[:, None],
            segment(south_lines[:, 2], back_x, across)[::-1][:, None],
        ],
        axis=1,
    )
    packed = packed.at[0].set(jnp.where(on_bottom, bottom_values, packed[0]))
    right_values = jnp.stack(
        [
            segment(north_lines[:, 1], start_y, rows_local),
            segment(south_lines[:, 1], back_y, rows_local)[::-1],
        ],
        axis=1,
    )
    packed = packed.at[:, -1, 4:6].set(jnp.where(on_right, right_values, packed[:, -1, 4:6]))
    left_values = jnp.stack(
        [
            segment(north_lines[:, 3], back_y, rows_local)[::-1],
            segment(south_lines[:, 3], start_y, rows_local),
        ],
        axis=1,
    )
    packed = packed.at[:, 0, 4:6].set(jnp.where(on_left, left_values, packed[:, 0, 4:6]))
    return packed


def fluid_columns(strips):
    return with_halo(strips, (("xi", 0),), 1, True)


def fluid_rows(strips):
    return with_halo(strips, (("eta", 0),), 1, False)


def fluid_lines(row_table, column_table):
    full_table = row_table.at[:, :, 1::2].add(column_table)
    return lax.psum(full_table, ("xi", "eta"))


def solid_columns(strips):
    return with_halo(strips, (("xi", 0),), 1, True)


def solid_rows(strips):
    return with_halo(strips, (("eta", 0),), 1, False)


def solid_lines(row_table, column_table):
    full_table = row_table.at[:, :, 1::2].add(column_table)
    return lax.psum(full_table, ("xi", "eta"))


def shards(
    mantle_disp,
    mantle_vel,
    mantle_acc,
    mantle_metric,
    mantle_moduli,
    mantle_rho,
    core_pot,
    core_rate,
    core_accel,
    core_metric,
    core_kappa,
    core_rho,
    inner_disp,
    inner_vel,
    inner_acc,
    inner_metric,
    inner_moduli,
    inner_rho,
):
    rows_local = mantle_disp.shape[1]
    across = 4 * EX + 1
    mantle_radial = 4 * MANTLE_LAYERS + 1
    core_radial = 4 * CORE_LAYERS + 1
    inner_radial = 4 * INNER_LAYERS + 1
    lateral = lateral_maps(EX)
    lumped_y, lumped_x = lumped_lines((rows_local - 1) // 4, EX)
    mantle_maps = radial_maps(MANTLE_LAYERS)
    core_maps = radial_maps(CORE_LAYERS)
    inner_maps = radial_maps(INNER_LAYERS)

    def blocked(grid_values, radial):
        return grid_values.reshape(grid_values.shape[:-2] + (rows_local, 1, across, 6, radial))

    half_square = 0.5 * time_step * time_step
    mantle_next = mantle_disp + time_step * mantle_vel + half_square * mantle_acc
    core_next = core_pot + time_step * core_rate + half_square * core_accel
    inner_next = inner_disp + time_step * inner_vel + half_square * inner_acc
    mantle_shape = blocked(mantle_next, mantle_radial)
    inner_shape = blocked(inner_next, inner_radial)
    core_geometry = blocked(core_metric, core_radial)
    face_lateral = lumped_y[:, None, None, None] * lumped_x[None, None, :, None]
    weight_top = face_lateral / (core_geometry[0][..., -1] * core_geometry[1][..., -1])
    weight_bottom = face_lateral / (core_geometry[0][..., 0] * core_geometry[1][..., 0])
    core_force = fluid_slab(core_next, core_metric, core_rho, lateral, core_maps, across)
    core_force = core_force.at[..., -1].add(weight_top * mantle_shape[2][..., 0])
    core_force = core_force.at[..., 0].add(-weight_bottom * inner_shape[2][..., -1])
    core_mass = blocked(
        native_volume(core_metric, lumped_y, lumped_x, core_maps) / core_kappa, core_radial
    )
    mantle_mass = blocked(
        mantle_rho * native_volume(mantle_metric, lumped_y, lumped_x, mantle_maps), mantle_radial
    )
    inner_mass = blocked(
        inner_rho * native_volume(inner_metric, lumped_y, lumped_x, inner_maps), inner_radial
    )
    mantle_width = 4 * mantle_radial
    core_packed = assemble(
        pack(jnp.stack([core_force, core_mass])), fluid_columns, fluid_rows, fluid_lines
    )
    core_sums = unpack(core_packed, 2, core_radial)
    core_acc_next = core_sums[0] / core_sums[1]
    mantle_force = elastic_slab(
        mantle_next, mantle_metric, mantle_moduli, lateral, mantle_maps, across
    )
    inner_force = elastic_slab(inner_next, inner_metric, inner_moduli, lateral, inner_maps, across)
    mantle_force = mantle_force.at[2, ..., 0].add(weight_top * core_acc_next[..., -1])
    inner_force = inner_force.at[2, ..., -1].add(-weight_bottom * core_acc_next[..., 0])
    solid = jnp.concatenate(
        [
            pack(jnp.concatenate([mantle_force, mantle_mass[None]])),
            pack(jnp.concatenate([inner_force, inner_mass[None]])),
        ],
        axis=-1,
    )
    solid = assemble(solid, solid_columns, solid_rows, solid_lines)
    mantle_sums = unpack(solid[..., :mantle_width], 4, mantle_radial)
    inner_sums = unpack(solid[..., mantle_width:], 4, inner_radial)
    mantle_acc_next = mantle_sums[:3] / mantle_sums[3]
    inner_acc_next = inner_sums[:3] / inner_sums[3]
    mantle_acc_next = mantle_acc_next.reshape(mantle_disp.shape)
    inner_acc_next = inner_acc_next.reshape(inner_disp.shape)
    core_acc_next = core_acc_next.reshape(core_pot.shape)
    half_step = 0.5 * time_step
    mantle_vel_next = mantle_vel + half_step * (mantle_acc + mantle_acc_next)
    core_rate_next = core_rate + half_step * (core_accel + core_acc_next)
    inner_vel_next = inner_vel + half_step * (inner_acc + inner_acc_next)
    return (
        mantle_next,
        mantle_vel_next,
        mantle_acc_next,
        core_next,
        core_rate_next,
        core_acc_next,
        inner_next,
        inner_vel_next,
        inner_acc_next,
    )


def solution(mesh):
    placed = (
        P(None, "eta", "xi"),
        P(None, "eta", "xi"),
        P(None, "eta", "xi"),
        P(None, "eta", "xi"),
        P(None, "eta", "xi"),
        P("eta", "xi"),
        P("eta", "xi"),
        P("eta", "xi"),
        P("eta", "xi"),
        P(None, "eta", "xi"),
        P("eta", "xi"),
        P("eta", "xi"),
        P(None, "eta", "xi"),
        P(None, "eta", "xi"),
        P(None, "eta", "xi"),
        P(None, "eta", "xi"),
        P(None, "eta", "xi"),
        P("eta", "xi"),
    )
    return jax.shard_map(
        shards,
        mesh=mesh,
        in_specs=placed,
        out_specs=(
            P(None, "eta", "xi"),
            P(None, "eta", "xi"),
            P(None, "eta", "xi"),
            P("eta", "xi"),
            P("eta", "xi"),
            P("eta", "xi"),
            P(None, "eta", "xi"),
            P(None, "eta", "xi"),
            P(None, "eta", "xi"),
        ),
        check_vma=False,
    )
```

profile of v0, /device:TPU:1, one launch (start us, length us, event | category | flops | bytes accessed | tf_op | source)
XLA Modules:
  0.0 926.9 jit_solution(14143932096653860439)
XLA Ops:
  18.8 6.5 collective-permute-start
  47.2 3.1 copy.3177
  50.3 2.7 fusion.130
  53.0 2.0 copy.3179
  55.0 11.0 %collective-permute-start.1 = (f32[1,17,6,18]{3,0,2,1:T(1,128)S(1)}, f32[1,17,6,18]{3,0,2,1:T(1,128)S(1)}, u32[]{:S(2)}, u32[]{:S(2)}) collective-permute-start(f32[1,17,6,18]{3,0,2,1:T(1,128)S(1)} %bitcast.601), channel_id=1, source_target_pairs={{16,0},{32,16},{48,32},{64,48},{80,64},{96,80},{112,96},{128,112},... | collective-permute-start | bytes 22040 | tf_op jit(solution)/shard_map/ppermute | solution.py:29
  71.5 2.2 slice_add_fusion.1
  73.7 10.2 %scatter-add.59 = f32[17,5,6,18]{1,0,3,2:T(8,128)S(1)} dynamic-update-slice(f32[17,5,6,18]{1,0,3,2:T(8,128)S(1)} %scatter-add.56, f32[17,1,6,18]{1,0,3,2:T(8,128)} %slice_add_fusion.1, s32[]{:T(128)} %constant.588.clone.1, s32[]{:T(128)} %constant.593.clone.1, s32[]{:T(128)} %constant.588.clone.1, s32[]{:T(128)} %constant.588.clone.1) | dynamic-update-slice | bytes 14692 | tf_op jit(solution)/shard_map/scatter-add | solution.py:257
  91.3 3.0 scatter-add.60
  94.3 3.0 scatter-add.61
  101.5 2.2 copy.3196
  105.2 2.8 dynamic_update_slice.83
  108.5 2.8 dynamic_update_slice.84
  112.7 2.8 dynamic_update_slice.76
  115.6 2.8 dynamic_update_slice.79
  118.4 2.8 dynamic_update_slice.80
  121.3 2.8 dynamic_update_slice.77
  125.3 10.9 %add.334 = f32[1,257,4,18]{1,0,3,2:T(1,128)S(1)} dynamic-update-slice(f32[1,257,4,18]{1,0,3,2:T(1,128)S(1)} %copy.3189, f32[1,5,4,18]{1,0,3,2:T(1,128)S(1)} %copy.3190, s32[]{:T(128)} %constant.588.clone.1, s32[]{:T(128)S(6)} %select_n.307, s32[]{:T(128)} %constant.588.clone.1, s32[]{:T(128)} %constant.588.clone.1) | dynamic-update-slice | bytes 2884 | tf_op jit(solution)/shard_map/add | solution.py:309
  136.1 10.9 %add.335 = f32[1,257,4,18]{1,0,3,2:T(1,128)S(1)} dynamic-update-slice(f32[1,257,4,18]{1,0,3,2:T(1,128)S(1)} %copy.3194, f32[1,5,4,18]{1,0,3,2:T(1,128)S(1)} %copy.3195, s32[]{:T(128)} %constant.588.clone.1, s32[]{:T(128)S(6)} %select_n.307, s32[]{:T(128)} %constant.588.clone.1, s32[]{:T(128)} %constant.588.clone.1) | dynamic-update-slice | bytes 2884 | tf_op jit(solution)/shard_map/add | solution.py:309
  149.5 292.2 %all-reduce.12.cloned.1.call-done = f32[2,257,4,18]{1,0,3,2:T(2,128)} async-done(((f32[2,257,4,18]{1,0,3,2:T(2,128)}), f32[2,257,4,18]{1,0,3,2:T(2,128)}) %all-reduce.12.cloned.1.call-update) | async-done | bytes 148048 | tf_op jit(solution)/shard_map/psum | solution.py:361
  444.2 3.0 scatter.26
  447.8 3.0 scatter.29
  451.9 2.8 scatter.30
  455.7 2.0 fusion.15
  467.2 2.8 fusion.11
  470.1 3.4 collective-permute-start.4
  475.4 2.1 collective-permute-start.5
  477.6 3.2 collective-permute-done.5
  480.9 2.2 copy.3264
  485.8 2.2 copy.3268
  490.7 4.7 fusion.3
  495.4 7.5 scatter-add.69
  502.8 5.7 slice_add_fusion
  508.6 22.1 %scatter-add.84 = f32[17,5,6,56]{1,3,2,0:T(8,128)S(1)} dynamic-update-slice(f32[17,5,6,56]{1,3,2,0:T(8,128)S(1)} %copy-done, f32[17,1,6,56]{1,3,2,0:T(8,128)} %slice_add_fusion, s32[]{:T(128)} %constant.588.clone.1, s32[]{:T(128)} %constant.593.clone.1, s32[]{:T(128)} %constant.588.clone.1, s32[]{:T(128)} %constant.588.clone.1) | dynamic-update-slice | bytes 45700 | tf_op jit(solution)/shard_map/scatter-add | solution.py:257
  530.8 3.2 collective-permute-start.6
  543.4 3.4 fusion.126
  546.8 3.9 copy.3371
  550.7 3.9 copy.3372
  571.5 2.3 add.352
  573.8 2.3 add.353
  578.1 2.7 scatter_fusion.1
  582.0 287.1 %all-reduce.14.cloned.1.call-done = f32[2,257,4,56]{1,3,2,0:T(8,128)} async-done(((f32[2,257,4,56]{1,3,2,0:T(8,128)}), f32[2,257,4,56]{1,3,2,0:T(8,128)}) %all-reduce.14.cloned.1.call-update) | async-done | bytes 460560 | tf_op jit(solution)/shard_map/psum | solution.py:374
  869.1 2.0 fusion.131
  885.6 2.3 slice_select_fusion.1
  887.9 6.4 scatter.36
  897.7 4.2 fusion.10
  901.9 5.4 scatter.39
  909.9 2.7 copy.3307
  914.4 2.2 copy.3302
  (601 shorter events, 132.3 us)
Async XLA Ops:
  7.2 434.5 %all-reduce.12.cloned.1.call-start = ((), (), s32[]{:S(2)}) async-start(), calls=%async_computation | async-start | bytes 442368 | tf_op jit(solution)/shard_map/psum | solution.py:361
  11.2 4.6 copy-start.33
  11.2 4.6 copy-start.34
  11.7 4.6 copy-start.24
  11.8 4.6 copy-start.26
  16.3 9.4 %copy-start.50 = (f32[17,1,5,6,1]{0,1,4,3,2:T(1,128)}, f32[17,1,5,6,1]{0,1,4,3,2:T(1,128)S(1)}, u32[]{:S(2)}) copy-start(f32[17,1,5,6,1]{0,1,4,3,2:T(1,128)S(1)} %get-tuple-element.455) | copy-start | bytes 6124
  16.4 15.1 %copy-start.23 = (f32[3,17,270]{2,0,1:T(4,128)}, f32[3,17,270]{2,0,1:T(4,128)S(1)}, u32[]{:S(2)}) copy-start(f32[3,17,270]{2,0,1:T(4,128)S(1)} %multiply_add_fusion.2) | copy-start | bytes 165244
  16.7 9.1 copy-start.57
  17.0 8.9 copy-start.38
  17.0 8.8 copy-start.29
  18.7 7.8 copy-start.65
  18.8 26.9 %collective-permute-start = (f32[1,17,6,18]{1,2,3,0:T(8,128)S(1)}, f32[1,17,6,18]{1,2,3,0:T(8,128)S(1)}, u32[]{:S(2)}, u32[]{:S(2)}) collective-permute-start(f32[1,17,6,18]{1,2,3,0:T(8,128)S(1)} %slice_bitcast_fusion.14), channel_id=1, source_target_pairs={{0,16},{16,32},{32,48},{48,64},{64,80},{80,96},{96,112},{112,128},... | collective-permute-start | bytes 22040 | tf_op jit(solution)/shard_map/ppermute | solution.py:27
  31.5 12.1 %copy-start.78 = (s32[2]{0:T(128)}, s32[2]{0:T(128)S(1)}, u32[]{:S(2)}) copy-start(s32[2]{0:T(128)S(1)} %iota_multiply_fusion) | copy-start | bytes 28
  38.7 4.9 copy-start.84
  55.0 13.4 %collective-permute-start.1 = (f32[1,17,6,18]{3,0,2,1:T(1,128)S(1)}, f32[1,17,6,18]{3,0,2,1:T(1,128)S(1)}, u32[]{:S(2)}, u32[]{:S(2)}) collective-permute-start(f32[1,17,6,18]{3,0,2,1:T(1,128)S(1)} %bitcast.601), channel_id=1, source_target_pairs={{16,0},{32,16},{48,32},{64,48},{80,64},{96,80},{112,96},{128,112},... | collective-permute-start | bytes 22040 | tf_op jit(solution)/shard_map/ppermute | solution.py:29
  73.7 14.2 %copy-start.19 = (f32[3,17,30,5]{2,1,3,0:T(8,128)S(1)}, f32[3,17,30,5]{2,1,3,0:T(8,128)}, u32[]{:S(2)}) copy-start(f32[3,17,30,5]{2,1,3,0:T(8,128)} %negate_bitcast_fusion.1) | copy-start | bytes 91804
  73.7 15.9 %copy-start.14 = (f32[3,17,30,9]{2,1,3,0:T(8,128)S(1)}, f32[3,17,30,9]{2,1,3,0:T(8,128)}, u32[]{:S(2)}) copy-start(f32[3,17,30,9]{2,1,3,0:T(8,128)} %negate_bitcast_fusion) | copy-start | bytes 165244
  73.7 16.2 %copy-start.41 = (f32[17,270]{1,0:T(8,128)S(1)}, f32[17,270]{1,0:T(8,128)}, u32[]{:S(2)}) copy-start(f32[17,270]{1,0:T(8,128)} %get-tuple-element.496) | copy-start | bytes 55084
  84.0 7.2 copy-start.55
  84.0 2.5 collective-permute-start.2
  86.6 7.7 collective-permute-start.3
  87.9 16.7 %copy-start.74 = (f32[17]{0:T(128)}, f32[17]{0:T(128)S(1)}, u32[]{:S(2)}) copy-start(f32[17]{0:T(128)S(1)} %or_convert_fusion) | copy-start | bytes 208
  98.8 13.3 %copy-start.70 = (f32[5]{0:T(128)S(1)}, f32[5]{0:T(128)}, u32[]{:S(2)}) copy-start(f32[5]{0:T(128)} %or_convert_fusion.1) | copy-start | bytes 64
  101.3 45.9 %copy-start.81 = (s32[2]{0:T(128)S(1)}, s32[2]{0:T(128)}, u32[]{:S(2)}) copy-start(s32[2]{0:T(128)} %add_bitcast_fusion) | copy-start | bytes 28
  103.7 45.2 %copy-start.79 = (s32[2]{0:T(128)S(1)}, s32[2]{0:T(128)}, u32[]{:S(2)}) copy-start(s32[2]{0:T(128)} %copy-done.78) | copy-start | bytes 28
  148.7 720.4 %all-reduce.14.cloned.1.call-start = ((), (), s32[]{:S(2)}) async-start(), calls=%async_computation.1 | async-start | bytes 1376256 | tf_op jit(solution)/shard_map/psum | solution.py:374
  454.8 5.6 copy-start.49
  454.8 5.6 copy-start.51
  454.8 5.6 copy-start.53
  454.8 5.6 copy-start.58
  470.1 7.4 collective-permute-start.4
  475.4 5.4 collective-permute-start.5
  484.8 5.9 copy-start.76
  495.4 7.5 copy-start.11
  502.8 5.7 copy-start
  508.6 27.9 %copy-start.36 = (f32[3,17,150]{2,0,1:T(4,128)S(1)}, f32[3,17,150]{2,0,1:T(4,128)}, u32[]{:S(2)}) copy-start(f32[3,17,150]{2,0,1:T(4,128)} %param.90) | copy-start | bytes 91804
  508.6 30.5 %copy-start.25 = (f32[3,17,270]{2,0,1:T(4,128)S(1)}, f32[3,17,270]{2,0,1:T(4,128)}, u32[]{:S(2)}) copy-start(f32[3,17,270]{2,0,1:T(4,128)} %param.78) | copy-start | bytes 165244
  508.6 31.6 %copy-start.27 = (f32[3,17,270]{2,0,1:T(4,128)S(1)}, f32[3,17,270]{2,0,1:T(4,128)}, u32[]{:S(2)}) copy-start(f32[3,17,270]{2,0,1:T(4,128)} %param.77) | copy-start | bytes 165244
  530.8 4.1 collective-permute-start.6
  535.1 6.3 copy-start.1
  535.2 8.0 collective-permute-start.7
  546.8 7.8 copy-start.75
  546.8 9.1 copy-start.71
  567.8 13.0 %copy-start.6 = (f32[17,5,6,2,9]{0,2,1,4,3:T(8,128)S(1)}, f32[17,5,6,2,9]{0,2,1,4,3:T(8,128)}, u32[]{:S(2)}) copy-start(f32[17,5,6,2,9]{0,2,1,4,3:T(8,128)} %copy-done.5) | copy-start | bytes 110164
  571.5 9.9 %copy-start.45 = (f32[17,270]{1,0:T(8,128)S(1)}, f32[17,270]{1,0:T(8,128)}, u32[]{:S(2)}) copy-start(f32[17,270]{1,0:T(8,128)} %param.84) | copy-start | bytes 55084
  571.5 9.9 %copy-start.47 = (f32[17,270]{1,0:T(8,128)S(1)}, f32[17,270]{1,0:T(8,128)}, u32[]{:S(2)}) copy-start(f32[17,270]{1,0:T(8,128)} %param.83) | copy-start | bytes 55084
  581.4 289.7 %copy-start.43 = (f32[17,270]{1,0:T(8,128)}, f32[17,270]{1,0:T(8,128)S(1)}, u32[]{:S(2)}) copy-start(f32[17,270]{1,0:T(8,128)S(1)} %div.140) | copy-start | bytes 55084
  909.9 4.6 copy-start.3
  (48 other events, 129.9 us)
Sparse Core Ops, SparseCore 0:
  148.8 292.8 all-reduce.11
  580.9 288.1 all-reduce.13
where the time goes:
time: 934 us; the launch traced here: 927 us
  waiting for transfers between devices  584 us (63%)
  local copies, waits for them, and re-layouts  229 us (25%)
  other arithmetic  54.7 us (6%)
  starting transfers between devices  30.3 us (3%)
  between operations  17.3 us (2%)
  matrix products  11.9 us (1%)
    psum x1, waiting for transfers between devices, fluid_lines(): return lax.psum(full_table, ('xi', 'eta'))  292 us
    psum x1, waiting for transfers between devices, solid_lines(): return lax.psum(full_table, ('xi', 'eta'))  287 us
    scatter-add x4, local copies, waits for them, and re-layouts, assemble(): packed = packed.at[:, 0].add(from_left).at[:, -1].add(from_right)  41.6 us
    dynamic_update_slice x16, local copies, waits for them, and re-layouts, place(): lax.dynamic_update_slice_in_dim(zero_line, jnp.where(active, edge_strip,...  24.8 us
  transfers between devices with their start and end apart: 10, of which 5 were waited for; matrix products, arithmetic and copies ran while one was open for 4% of the time, Pallas kernels for 0%

commit v1 on v0

v1 whole, which is shorter than its diff:
```python
import functools
import math

import jax
import jax.numpy as jnp
import numpy as np
from jax import lax
from jax.experimental import pallas as pl
from jax.experimental.pallas import tpu as pltpu
from jax.sharding import PartitionSpec as P

MESH = pl.DeviceIdType.MESH
F32 = jnp.float32
STEP = 0.1
HALF_SQUARE = 0.5 * STEP * STEP
HALF_STEP = 0.5 * STEP
ROWS = 17
PAD = 24
LANES = 128
SHIFTS = (-4, -3, -2, -1, 1, 2, 3, 4)
FORWARD, ADJOINT, MEAN, SPLIT, CENTRE, JUMP, LUMPED, TABLE = 0, 8, 16, 17, 18, 19, 20, 24


def gll_tables():
    radical = math.sqrt(3.0 / 7.0)
    points = np.array([-1.0, -radical, 0.0, radical, 1.0])
    weights = np.array([0.1, 49.0 / 90.0, 32.0 / 45.0, 49.0 / 90.0, 0.1])
    slopes = np.zeros((5, 5))
    products = np.array([np.prod([points[a] - points[c] for c in range(5) if c != a]) for a in range(5)])
    for a in range(5):
        for b in range(5):
            if a == b:
                slopes[a, b] = np.sum([1.0 / (points[a] - points[c]) for c in range(5) if c != a])
            else:
                slopes[a, b] = products[a] / (products[b] * (points[a] - points[b]))
    return weights, slopes


WEIGHTS, SLOPES = gll_tables()


def line_table(elements):
    count = 4 * elements + 1
    table = np.zeros((TABLE, count))
    shared = [p % 4 == 0 and 0 < p < count - 1 for p in range(count)]
    for p in range(count):
        for at, s in enumerate(SHIFTS):
            q = p + s
            if not 0 <= q < count:
                continue
            e = min(p, q) // 4
            a, b = p - 4 * e, q - 4 * e
            if max(a, b) > 4:
                continue
            table[FORWARD + at, p] = SLOPES[a, b]
            table[ADJOINT + at, p] = SLOPES[b, a] * (0.5 if shared[q] else 1.0)
        table[MEAN, p] = 0.5 if shared[p] else 1.0
        table[SPLIT, p] = 0.5 if shared[p] else 0.0
        if shared[p]:
            table[CENTRE, p] = 0.5 * (SLOPES[4, 4] + SLOPES[0, 0])
            table[JUMP, p] = 0.5 * (SLOPES[4, 4] - SLOPES[0, 0])
            table[LUMPED, p] = WEIGHTS[0] + WEIGHTS[4]
        else:
            a = 4 if p == count - 1 else p % 4
            table[CENTRE, p] = SLOPES[a, a]
            table[LUMPED, p] = WEIGHTS[a]
    return table


def coefficient_tables():
    rows = np.zeros((TABLE, PAD))
    rows[LUMPED] = 1.0
    rows[:, :ROWS] = line_table(4)
    rows = np.broadcast_to(rows[:, :, None], (TABLE, PAD, LANES))
    lanes = np.zeros((TABLE, LANES))
    lanes[LUMPED] = 1.0
    lanes[:, :54] = np.tile(line_table(2), (1, 6))
    lanes[:, 54:84] = np.tile(line_table(1), (1, 6))
    return np.asarray(rows, np.float32), np.asarray(lanes, np.float32)


def lane_index(shape):
    return lax.broadcasted_iota(jnp.int32, shape, len(shape) - 1)


def turn(values, amount, axis):
    amount = amount % values.shape[axis]
    return values if amount == 0 else pltpu.roll(values, amount, axis)


def slope_pair(values, table, axis):
    below = above = None
    for at, s in enumerate(SHIFTS):
        term = table(FORWARD + at) * turn(values, -s, axis)
        if s < 0:
            below = term if below is None else below + term
        else:
            above = term if above is None else above + term
    mean = table(MEAN) * (below + above) + table(CENTRE) * values
    half_jump = table(SPLIT) * (below - above) + table(JUMP) * values
    return mean, half_jump


def adjoint_pair(mean, half_jump, table, axis):
    first, second = mean + half_jump, mean - half_jump
    total = table(CENTRE) * mean + table(JUMP) * half_jump
    for at, s in enumerate(SHIFTS):
        total = total + table(ADJOINT + at) * turn(first if s > 0 else second, -s, axis)
    return total


def slope_x(values):
    return jnp.stack([sum(float(SLOPES[a, b]) * values[b] for b in range(5) if abs(SLOPES[a, b]) > 1e-12) for a in range(5)])


def adjoint_x(flux):
    return jnp.stack([sum(float(SLOPES[b, a]) * flux[b] for b in range(5) if abs(SLOPES[b, a]) > 1e-12) for a in range(5)])


def slabs(outer, inner, fill):
    lane = lane_index((PAD, LANES))
    parts = []
    for x in range(5):
        part = jnp.where(lane < 54, turn(outer, -54 * x, 1)[:, :LANES], fill)
        if inner is not None:
            other = turn(inner, 54 - 30 * x, 1)[:, :LANES]
            part = jnp.where((lane >= 54) & (lane < 84), other, part)
        parts.append(part)
    return jnp.stack(parts)


def widen(pad, values):
    pad[0:ROWS, 0 : values.shape[-1]] = values
    return pad[...]


def local_phase(ins, disp_outs, store_tile, scratch):
    (md, mv, ma, mg, mm, mr, cp, cr, ca, cg, ck, crho, nd, nv, na, ng, nm, nr, row_table, lane_table) = ins
    md_new, cp_new, nd_new = disp_outs
    wide, narrow = scratch

    def rows(index):
        return row_table[index][None]

    def lanes(index):
        return lane_table[index : index + 1, :][None]

    wide[...] = jnp.ones_like(wide)
    narrow[...] = jnp.ones_like(narrow)
    displace = []
    for i in range(3):
        outer = md[i] + STEP * mv[i] + HALF_SQUARE * ma[i]
        inner = nd[i] + STEP * nv[i] + HALF_SQUARE * na[i]
        md_new[i] = outer
        nd_new[i] = inner
        displace.append(slabs(widen(wide, outer), widen(narrow, inner), 0.0))
    row = lax.broadcasted_iota(jnp.int32, (PAD, LANES), 0)
    displace = [jnp.where((row < ROWS)[None], u, 0.0) for u in displace]
    scale = [slabs(widen(wide, mg[i]), widen(narrow, ng[i]), 1.0) for i in range(3)]
    lam, mu = [slabs(widen(wide, mm[i]), widen(narrow, nm[i]), 1.0) for i in range(2)]
    density = slabs(widen(wide, mr[...]), widen(narrow, nr[...]), 1.0)
    row_column = jnp.stack([row_table[LUMPED] * float(WEIGHTS[x]) for x in range(5)])
    weight = row_column * lanes(LUMPED)
    volume = weight / (scale[0] * scale[1] * scale[2])
    store_tile(3, density * volume)

    pull = [volume * scale[m] for m in range(3)]
    along_y, along_x, along_r, jump_y, jump_r = [], [], [], [], []
    for i in range(3):
        mean, half = slope_pair(displace[i], rows, 1)
        along_y.append(scale[0] * mean)
        jump_y.append(scale[0] * half)
        along_x.append(scale[1] * slope_x(displace[i]))
        mean, half = slope_pair(displace[i], lanes, 2)
        along_r.append(scale[2] * mean)
        jump_r.append(scale[2] * half)
    spread = lam * (along_y[0] + along_x[1] + along_r[2])
    stiff = lam + 2.0 * mu
    shear_yx = mu * (along_x[0] + along_y[1])
    shear_yr = mu * (along_r[0] + along_y[2])
    shear_xr = mu * (along_r[1] + along_x[2])
    stress_y = [spread + 2.0 * mu * along_y[0], shear_yx, shear_yr]
    stress_x = [shear_yx, spread + 2.0 * mu * along_x[1], shear_xr]
    stress_r = [shear_yr, shear_xr, spread + 2.0 * mu * along_r[2]]
    for i in range(3):
        total = adjoint_pair(pull[0] * stress_y[i], pull[0] * (stiff if i == 0 else mu) * jump_y[i], rows, 1)
        total = total + adjoint_x(pull[1] * stress_x[i])
        total = total + adjoint_pair(pull[2] * stress_r[i], pull[2] * (stiff if i == 2 else mu) * jump_r[i], lanes, 2)
        store_tile(i, -total)

    outer = cp[...] + STEP * cr[...] + HALF_SQUARE * ca[...]
    cp_new[...] = outer
    potential = jnp.where((row < ROWS)[None], slabs(widen(wide, outer), None, 0.0), 0.0)
    scale = [slabs(widen(wide, cg[i]), None, 1.0) for i in range(3)]
    kappa = slabs(widen(wide, ck[...]), None, 1.0)
    density = slabs(widen(wide, crho[...]), None, 1.0)
    face = row_column / (scale[0] * scale[1])
    volume = face * lanes(LUMPED) / scale[2]
    mass = volume / kappa
    thin = volume / density
    pull = [thin * scale[m] * scale[m] for m in range(3)]
    mean, half = slope_pair(potential, rows, 1)
    total = adjoint_pair(pull[0] * mean, pull[0] * half, rows, 1)
    total = total + adjoint_x(pull[1] * slope_x(potential))
    mean, half = slope_pair(potential, lanes, 2)
    total = total + adjoint_pair(pull[2] * mean, pull[2] * half, lanes, 2)
    lane = lane_index((1, PAD, LANES))
    is_top = (lane < 54) & (lane % 9 == 8)
    is_bottom = (lane < 54) & (lane % 9 == 0)
    above = turn(displace[2], 8, 2)
    below = jnp.zeros_like(above)
    for k in range(6):
        below = jnp.where(lane == 9 * k, turn(displace[2], 4 * k - 58, 2), below)
    force = jnp.where(is_top, face * above, 0.0) - jnp.where(is_bottom, face * below, 0.0) - total
    store_tile(4, jnp.where(lane < 54, force, turn(mass, 54, 2)))
    store_tile(5, jnp.where(is_top | is_bottom, face, 0.0))


def group_masks(shape):
    lane = lane_index(shape)
    field = lax.broadcasted_iota(jnp.int32, shape, len(shape) - 2)
    nine, five = [], []
    for k in range(6):
        first = (lane >= 9 * k) & (lane < 9 * k + 9)
        second = (lane >= 54 + 9 * k) & (lane < 63 + 9 * k) & (field == 4)
        nine.append(first | second)
        five.append((lane >= 54 + 5 * k) & (lane < 59 + 5 * k) & (field < 4))
    return nine, five


def move_groups(values, pairs, masks):
    nine, five = masks
    axis = values.ndim - 1
    result = jnp.zeros_like(values)
    for distance in sorted({b - a for a, b in pairs}):
        long, short = turn(values, 9 * distance, axis), turn(values, 5 * distance, axis)
        for a, b in pairs:
            if b - a == distance:
                result = jnp.where(nine[b], long, jnp.where(five[b], short, result))
    return result


FROM_LEFT = ((3, 0), (0, 1), (1, 2), (2, 3))
FROM_RIGHT = ((1, 0), (2, 1), (3, 2), (0, 3))


def exchange_phase(n_xi, n_eta, z, bufs, sems, before_send=None):
    col_left, col_right, row_below, row_above, mirror, slots, polar, polar_extra, edge_rows = bufs
    send, recv = sems
    I, J = lax.axis_index("xi"), lax.axis_index("eta")
    last_i, last_j = n_xi - 1, n_eta - 1
    left, right = lax.rem(I + n_xi - 1, n_xi), lax.rem(I + 1, n_xi)
    down, up = lax.rem(J + n_eta - 1, n_eta), lax.rem(J + 1, n_eta)
    top = J // last_j
    far = I // last_i
    quarter = I // 4
    j_right = top * quarter + (1 - top) * (last_j - quarter)
    j_left = (1 - top) * quarter + top * (last_j - quarter)
    lean = (2 * ((I % 4) // 3) - 1) * (2 * top - 1)
    at_edge = J % last_j == 0
    at_side = I % last_i == 0
    has_extra = ((I + 1) % 4) // 2 == 0

    def i_top(q):
        return far * (4 * J + q) + (1 - far) * (last_i - 4 * J - q)

    def i_bottom(q):
        return (1 - far) * (4 * J + q) + far * (last_i - 4 * J - q)

    def copy(src, dst, s, r, device):
        return pltpu.make_async_remote_copy(
            src_ref=src, dst_ref=dst, send_sem=send.at[s], recv_sem=recv.at[r], device_id=device, device_id_type=MESH
        )

    def main_copies():
        copies = []
        for q in range(4):
            src = z.at[4 * far, pl.ds(4 * q, 5)]
            dst = polar.at[1 - far]
            copies.append((copy(src, dst, 7 + q, 13 + 1 - far, (i_top(q), last_j)), J != last_j if q == 3 else None))
            copies.append((copy(src, dst, 11 + q, 13 + 1 - far, (i_bottom(q), 0)), J != 0 if q == 0 else None))
        for q, y, s, exists in ((-1, 0, 15, J != 0), (4, 16, 17, J != last_j)):
            src = z.at[4 * far, y]
            dst = polar_extra.at[1 - far]
            copies.append((copy(src, dst, s, 15 + 1 - far, (i_top(q), last_j)), exists))
            copies.append((copy(src, dst, s + 1, 15 + 1 - far, (i_bottom(q), 0)), exists))
        return copies

    def guarded(condition, action):
        if condition is None:
            action()
        else:
            pl.when(condition)(action)

    barrier = pltpu.get_barrier_semaphore()

    def greet(i, j):
        pl.semaphore_signal(barrier, inc=1, device_id=(i, j), device_id_type=MESH)

    greet(left, J)
    greet(right, J)
    greet(I, down)
    greet(I, up)

    @pl.when(at_edge)
    def _():
        greet(last_i - I, J)
        pl.when(I != last_i)(lambda: greet(last_i, j_right))
        pl.when(I != 0)(lambda: greet(0, j_left))

        @pl.when(has_extra)
        def _():
            @pl.when(I % last_i != 0)
            def _():
                greet(last_i, j_right + lean)
                greet(0, j_left - lean)

    @pl.when(at_side)
    def _():
        for q in range(4):
            guarded(J != last_j if q == 3 else None, functools.partial(greet, i_top(q), last_j))
            guarded(J != 0 if q == 0 else None, functools.partial(greet, i_bottom(q), 0))

    if before_send is not None:
        before_send()

    bottom, near = (last_j - J) // last_j, (last_i - I) // last_i
    partners = 4 + (top + bottom) * (3 - far - near) + (far + near) * (12 - 3 * top - 3 * bottom)
    pl.semaphore_wait(barrier, partners)

    to_left = copy(z.at[0], col_right, 0, 1, (left, J))
    to_right = copy(z.at[4], col_left, 1, 0, (right, J))
    to_left.start()
    to_right.start()

    @pl.when(at_side)
    def _():
        for item, condition in main_copies():
            guarded(condition, item.start)
        pl.when(J == last_j)(lambda: polar.__setitem__(1 - far, z[4 * far, pl.ds(12, 5)]))
        pl.when(J == 0)(lambda: polar.__setitem__(1 - far, z[4 * far, pl.ds(0, 5)]))

    masks = group_masks((8, LANES))
    for end, y in ((0, 0), (1, 16)):
        for x in range(1, 4):
            edge_rows[end, x] = z[x, y]
    to_right.wait_recv()
    for end, y in ((0, 0), (1, 16)):
        got = col_left[y]
        got = jnp.where(I == 0, move_groups(got, FROM_LEFT, masks), got)
        edge_rows[end, 0] = z[0, y] + got
    to_left.wait_recv()
    for end, y in ((0, 0), (1, 16)):
        got = col_right[y]
        got = jnp.where(I == last_i, move_groups(got, FROM_RIGHT, masks), got)
        edge_rows[end, 4] = z[4, y] + got

    to_up = copy(edge_rows.at[1], row_below, 2, 2, (I, up))
    to_down = copy(edge_rows.at[0], row_above, 3, 3, (I, down))
    to_mirror = copy(edge_rows.at[top], mirror, 4, 4, (last_i - I, J))
    slot = slots.at[top, I % 4]
    to_far = copy(edge_rows.at[top], slot, 5, 5 + 4 * top + I % 4, (last_i, j_right))
    to_near = copy(edge_rows.at[top], slot, 6, 5 + 4 * top + I % 4, (0, j_left))

    @pl.when(at_edge)
    def _():
        to_mirror.start()
        pl.when(I != last_i)(to_far.start)
        pl.when(I != 0)(to_near.start)
        pl.when(I % last_i == 0)(lambda: slots.__setitem__((top, I % 4), edge_rows[top]))

    to_up.start()
    to_down.start()

    to_up.wait_recv()
    to_down.wait_recv()

    @pl.when(at_edge)
    def _():
        to_mirror.wait_recv()
        for k in range(2):
            main = copy(z.at[0, pl.ds(0, 5)], polar.at[k], 7, 13 + k, (left, J))
            pl.when(I != (last_i if k == 0 else 0))(main.wait_recv)

        @pl.when(has_extra)
        def _():
            @pl.when(I % last_i != 0)
            def _():
                for k in range(2):
                    copy(z.at[0, 0], polar_extra.at[k], 15, 15 + k, (left, J)).wait_recv()

    @pl.when(at_side)
    def _():
        for end in range(2):
            for j in range(4):
                arrival = copy(edge_rows.at[0], slots.at[end, j], 5, 5 + 4 * end + j, (left, J))
                if j in (0, 3):
                    away = (J - end * last_j) * (J - end * last_j) + (3 * far - j) * (3 * far - j)
                    pl.when(away != 0)(arrival.wait_recv)
                else:
                    arrival.wait_recv()

    to_left.wait_send()
    to_right.wait_send()
    to_up.wait_send()
    to_down.wait_send()

    @pl.when(at_edge)
    def _():
        to_mirror.wait_send()
        pl.when(I != last_i)(to_far.wait_send)
        pl.when(I != 0)(to_near.wait_send)

    @pl.when(at_side)
    def _():
        for item, condition in main_copies():
            guarded(condition, item.wait_send)


EXCHANGE_SHAPES = (
    (17, 8, LANES),
    (17, 8, LANES),
    (5, 8, LANES),
    (5, 8, LANES),
    (5, 8, LANES),
    (2, 4, 5, 8, LANES),
    (2, 5, 8, LANES),
    (2, 8, LANES),
)
EDGE_SHAPE = (2, 5, 8, LANES)
SENDS, RECEIVES = 19, 17


def total_phase(n_xi, n_eta, work, bufs):
    col_left, col_right, row_below, row_above, mirror, slots, polar, polar_extra = bufs
    I, J = lax.axis_index("xi"), lax.axis_index("eta")
    last_i, last_j = n_xi - 1, n_eta - 1
    far = I // last_i
    masks = group_masks((8, LANES))
    big_masks = group_masks((17, 8, LANES))

    def span(x, y):
        return pl.ds(8 * (17 * x + y), 8)

    def add(x, y, values):
        work[span(x, y), :] += values

    def add_column(x, values):
        work[pl.ds(8 * 17 * x, 8 * 17), :] += values.reshape(8 * 17, LANES)

    @pl.when(I != 0)
    def _():
        add_column(0, col_left[...])

    @pl.when(I != last_i)
    def _():
        add_column(4, col_right[...])

    @pl.when(I == 0)
    def _():
        add_column(0, move_groups(col_left[...], FROM_LEFT, big_masks))

    @pl.when(I == last_i)
    def _():
        add_column(4, move_groups(col_right[...], FROM_RIGHT, big_masks))

    @pl.when(J != last_j)
    def _():
        for x in range(5):
            add(x, 16, row_above[x])

    @pl.when(J != 0)
    def _():
        for x in range(5):
            add(x, 0, row_below[x])

    for end, y, pole, ring, ring_pairs in (
        (1, 16, 4, row_above, ((4, 0), (0, 5))),
        (0, 0, 5, row_below, ((5, 0), (0, 4))),
    ):

        @pl.when(J == end * last_j)
        def _():
            for x in range(5):
                value = move_groups(ring[x], ring_pairs, masks)
                value = value + move_groups(mirror[4 - x], ((2, pole), (pole, 2)), masks)
                value = value + move_groups(polar[0, x if end == 1 else 4 - x], ((pole, 1),), masks)
                value = value + move_groups(polar[1, 4 - x if end == 1 else x], ((pole, 3),), masks)
                add(x, y, value)

            def extra(x):
                value = move_groups(polar_extra[0], ((pole, 1),), masks)
                add(x, y, value + move_groups(polar_extra[1], ((pole, 3),), masks))

            @pl.when(I % last_i != 0)
            def _():
                pl.when(I % 4 == 0)(lambda: extra(0))
                pl.when(I % 4 == 3)(lambda: extra(4))

    for side in range(2):

        @pl.when(I == side * last_i)
        def _():
            group = 1 if side == 1 else 3
            for end in range(2):
                pole = 4 if end == 1 else 5
                forward = side == end
                for y in range(17):
                    point = y if forward else 16 - y
                    j, x = min(point // 4, 3), point - 4 * min(point // 4, 3)

                    def place(y=y, j=j, x=x):
                        add(4 * side, y, move_groups(slots[end, j, x], ((group, pole),), masks))

                    if y == 0:
                        pl.when(J != 0)(place)
                    elif y == 16:
                        pl.when(J != last_j)(place)
                    else:
                        place()


def output_phase(load_tile, ins, outs):
    mv, ma, cr, ca, nv, na = ins
    mv_new, ma_new, cr_new, ca_new, nv_new, na_new = outs
    lane = lane_index((1, ROWS, LANES))
    core = load_tile(4)
    accel = core / turn(core, -54, 2)
    push = load_tile(5) * accel
    force = load_tile(2)
    force = force + jnp.where((lane < 54) & (lane % 9 == 0), turn(push, -8, 2), 0.0)
    for k in range(6):
        force = force - jnp.where(lane == 58 + 5 * k, turn(push, 58 - 4 * k, 2), 0.0)
    mass = load_tile(3)

    def gather(values, start, count, width):
        lanes_out = lane_index((ROWS, width))
        blank = jnp.zeros((ROWS, width - LANES), F32)
        result = None
        for x in range(5):
            moved = turn(jnp.concatenate([values[x], blank], axis=1), count * x - start, 1)
            result = moved if result is None else jnp.where(lanes_out >= count * x, moved, result)
        return result

    for i in range(3):
        new = (force if i == 2 else load_tile(i)) / mass
        outer = gather(new, 0, 54, 384)[:, :270]
        ma_new[i] = outer
        mv_new[i] = mv[i] + HALF_STEP * (ma[i] + outer)
        inner = gather(new, 54, 30, 256)[:, :150]
        na_new[i] = inner
        nv_new[i] = nv[i] + HALF_STEP * (na[i] + inner)
    outer = gather(accel, 0, 54, 384)[:, :270]
    ca_new[...] = outer
    cr_new[...] = cr[...] + HALF_STEP * (ca[...] + outer)


def local_kernel(*refs):
    ins, disp_outs, z, scratch = refs[:20], refs[20:23], refs[23], refs[24:]
    z[...] = jnp.zeros_like(z)

    def store_tile(t, values):
        for x in range(5):
            z[pl.ds(8 * ROWS * x + t, ROWS, stride=8), :] = values[x, :ROWS]

    local_phase(ins, disp_outs, store_tile, scratch)


def exchange_kernel(n_xi, n_eta, z, *refs):
    bufs, (edge_rows, send, recv) = refs[:8], refs[8:]
    exchange_phase(n_xi, n_eta, z, bufs + (edge_rows,), (send, recv))


def output_kernel(n_xi, n_eta, *refs):
    z, bufs, ins, outs, work = refs[0], refs[1:9], refs[9:15], refs[15:21], refs[21]
    work[...] = z[...]
    total_phase(n_xi, n_eta, work, bufs)

    def load_tile(t):
        return jnp.stack([work[pl.ds(8 * ROWS * x + t, ROWS, stride=8), :] for x in range(5)])

    output_phase(load_tile, ins, outs)


def solution(mesh):
    n_xi, n_eta = mesh.shape["xi"], mesh.shape["eta"]
    row_table, lane_table = coefficient_tables()
    vmem = pl.BlockSpec(memory_space=pltpu.VMEM)

    def shape(*dims):
        return jax.ShapeDtypeStruct(dims, F32)

    def step(md, mv, ma, mg, mm, mr, cp, cr, ca, cg, ck, crho, nd, nv, na, ng, nm, nr):
        ins = (md, mv, ma, mg, mm, mr, cp, cr, ca, cg, ck, crho, nd, nv, na, ng, nm, nr)
        big, thin, small = shape(*md.shape), shape(*cp.shape), shape(*nd.shape)
        md_new, cp_new, nd_new, z = pl.pallas_call(
            local_kernel,
            out_shape=(big, thin, small, shape(5 * ROWS * 8, LANES)),
            in_specs=[vmem] * 20,
            out_specs=[vmem] * 4,
            scratch_shapes=[pltpu.VMEM((PAD, 384), F32), pltpu.VMEM((PAD, 256), F32)],
            compiler_params=pltpu.CompilerParams(vmem_limit_bytes=32 * 1024 * 1024),
        )(*ins, jnp.asarray(row_table), jnp.asarray(lane_table))
        bufs = pl.pallas_call(
            functools.partial(exchange_kernel, n_xi, n_eta),
            out_shape=tuple(shape(*dims) for dims in EXCHANGE_SHAPES),
            in_specs=[vmem],
            out_specs=[vmem] * 8,
            scratch_shapes=[
                pltpu.VMEM(EDGE_SHAPE, F32),
                pltpu.SemaphoreType.DMA((SENDS,)),
                pltpu.SemaphoreType.DMA((RECEIVES,)),
            ],
            compiler_params=pltpu.CompilerParams(
                collective_id=0, has_side_effects=True, vmem_limit_bytes=32 * 1024 * 1024
            ),
        )(z.reshape(5, ROWS, 8, LANES))
        mv_new, ma_new, cr_new, ca_new, nv_new, na_new = pl.pallas_call(
            functools.partial(output_kernel, n_xi, n_eta),
            out_shape=(big, big, thin, thin, small, small),
            in_specs=[vmem] * 15,
            out_specs=[vmem] * 6,
            scratch_shapes=[pltpu.VMEM((5 * ROWS * 8, LANES), F32)],
            compiler_params=pltpu.CompilerParams(vmem_limit_bytes=32 * 1024 * 1024),
        )(z, *bufs, mv, ma, cr, ca, nv, na)
        return md_new, mv_new, ma_new, cp_new, cr_new, ca_new, nd_new, nv_new, na_new

    wide, thin = P(None, "eta", "xi"), P("eta", "xi")
    return jax.shard_map(
        step,
        mesh=mesh,
        in_specs=(wide,) * 5 + (thin,) * 4 + (wide,) + (thin,) * 2 + (wide,) * 5 + (thin,),
        out_specs=(wide,) * 3 + (thin,) * 3 + (wide,) * 3,
        check_vma=False,
    )
```

time: 934 us -> 51 us (0.05)
  the two profiles are of different devices: /device:TPU:1 before, /device:TPU:2 now
where the time goes in v1:
time: 51 us; the launch traced here: 50.6 us
  Pallas kernels  37.9 us (74%)
  local copies, waits for them, and re-layouts  11.9 us (23%)
  between operations  0.8 us (2%)
    pallas_call x1, Pallas kernels, step(): pl.pallas_call(functools.partial(exchange_kernel, n_xi, n_eta), out_shape...  33.4 us
    unnamed x55, local copies, waits for them, and re-layouts  11.9 us
    pallas_call x1, Pallas kernels, step(): pl.pallas_call(local_kernel, out_shape=(big, thin, small, shape(5 * ROWS...  2.83 us
    pallas_call x1, Pallas kernels, step(): pl.pallas_call(functools.partial(output_kernel, n_xi, n_eta), out_shape=(...  1.7 us

profile of v1, /device:TPU:2, one launch (start us, length us, event | category | flops | bytes accessed | tf_op | source)
XLA Modules:
  0.0 50.6 jit_solution(3918271123854308536)
XLA Ops:
  0.6 0.0 copy-start.14
  0.7 0.8 %copy.39.refs_16_ = f32[2,17,150]{2,1,0:T(8,128)S(1)} copy(f32[2,17,150]{2,0,1:T(2,128)} %param.36) | data formatting | bytes 40800 | tf_op args[16]
  1.5 0.1 copy-done.14
  1.5 0.0 copy-start.15
  1.5 0.9 %copy-done.15 = f32[3,17,150]{2,0,1:T(4,128)S(1)} copy-done((f32[3,17,150]{2,0,1:T(4,128)S(1)}, f32[3,17,150]{2,0,1:T(4,128)}, u32[]{:S(2)}) %copy-start.15) | copy-done | bytes 30624
  2.4 0.0 copy-start.18
  2.4 0.8 %copy-done.18 = f32[2,17,270]{2,0,1:T(2,128)S(1)} copy-done((f32[2,17,270]{2,0,1:T(2,128)S(1)}, f32[2,17,270]{2,0,1:T(2,128)}, u32[]{:S(2)}) %copy-start.18) | copy-done | bytes 36744
  3.2 0.0 copy-start.16
  3.2 0.9 %copy-done.16 = f32[3,17,150]{2,0,1:T(4,128)S(1)} copy-done((f32[3,17,150]{2,0,1:T(4,128)S(1)}, f32[3,17,150]{2,0,1:T(4,128)}, u32[]{:S(2)}) %copy-start.16) | copy-done | bytes 30624
  4.1 0.0 copy-start.17
  4.1 0.9 %copy-done.17 = f32[3,17,150]{2,0,1:T(4,128)S(1)} copy-done((f32[3,17,150]{2,0,1:T(4,128)S(1)}, f32[3,17,150]{2,0,1:T(4,128)}, u32[]{:S(2)}) %copy-start.17) | copy-done | bytes 30624
  5.0 0.0 copy-start.9
  5.0 0.9 %copy-done.9 = f32[3,17,270]{2,0,1:T(4,128)S(1)} copy-done((f32[3,17,270]{2,0,1:T(4,128)S(1)}, f32[3,17,270]{2,0,1:T(4,128)}, u32[]{:S(2)}) %copy-start.9) | copy-done | bytes 55104
  5.9 0.0 copy-start.10
  5.9 0.0 copy-start.13
  5.9 0.9 %copy-done.10 = f32[3,17,270]{2,0,1:T(4,128)S(1)} copy-done((f32[3,17,270]{2,0,1:T(4,128)S(1)}, f32[3,17,270]{2,0,1:T(4,128)}, u32[]{:S(2)}) %copy-start.10) | copy-done | bytes 55104
  6.8 0.0 copy-start.11
  6.8 0.0 copy-start.12
  6.8 0.9 %copy-done.11 = f32[3,17,270]{2,0,1:T(4,128)S(1)} copy-done((f32[3,17,270]{2,0,1:T(4,128)S(1)}, f32[3,17,270]{2,0,1:T(4,128)}, u32[]{:S(2)}) %copy-start.11) | copy-done | bytes 55104
  7.7 0.0 copy-start
  7.7 0.0 copy-done.12
  7.7 0.0 copy-start.6
  7.7 0.0 copy-start.8
  7.7 0.0 copy-done.13
  7.7 0.0 copy-start.1
  7.8 0.0 copy-start.2
  7.8 0.0 copy-start.3
  7.8 0.0 copy-start.4
  7.8 0.0 copy-start.5
  7.8 0.0 copy-start.7
  7.8 0.8 %copy-done = f32[24,24,128]{2,1,0:T(8,128)S(1)} copy-done((f32[24,24,128]{2,1,0:T(8,128)S(1)}, f32[24,24,128]{2,1,0:T(8,128)}, u32[]{:S(2)}) %copy-start) | copy-done | bytes 294936
  8.6 0.0 copy-done.6
  8.6 0.0 copy-done.8
  8.6 0.0 copy-done.1
  8.6 0.0 copy-done.2
  8.6 0.0 copy-done.3
  8.7 0.0 copy-done.4
  8.7 0.0 copy-done.5
  8.7 0.0 copy-done.7
  8.7 2.8 %shard_map.259 = (f32[3,17,270]{2,1,0:T(8,128)S(1)}, f32[17,270]{1,0:T(8,128)}, f32[3,17,150]{2,1,0:T(8,128)S(1)}, f32[680,128]{1,0:T(8,128)S(1)}) custom-call(f32[3,17,270]{2,1,0:T(8,128)S(1)} %copy.29.refs_0_, f32[3,17,270]{2,1,0:T(8,128)S(1)} %copy.30.refs_1_.refs_9_, f32[3,17,270]{2,1,0:T(8,128)S(1)} %copy.31.refs_2_.refs_10_, ...), custom_call_target="tpu_custom_call" | custom-call | tf_op jit(solution)/shard_map/pallas_call | solution.py:596
  11.5 0.7 %copy.44 = f32[3,17,270]{2,0,1:T(4,128)} copy(f32[3,17,270]{2,1,0:T(8,128)S(1)} %get-tuple-element.45) | data formatting | bytes 110160
  12.2 0.7 %copy.47 = f32[3,17,150]{2,0,1:T(4,128)} copy(f32[3,17,150]{2,1,0:T(8,128)S(1)} %get-tuple-element.51) | data formatting | bytes 61200
  12.8 33.4 %shard_map.260 = (f32[17,8,128]{2,1,0:T(8,128)S(1)}, f32[17,8,128]{2,1,0:T(8,128)S(1)}, f32[5,8,128]{2,1,0:T(8,128)S(1)}, f32[5,8,128]{2,1,0:T(8,128)S(1)}, f32[...) custom-call(f32[5,17,8,128]{3,2,1,0:T(8,128)S(1)} %bitcast.1), custom_call_target="tpu_custom_call" | custom-call | tf_op jit(solution)/shard_map/pallas_call | solution.py:604
  46.2 1.7 %shard_map.261 = (f32[3,17,270]{2,1,0:T(8,128)S(1)}, f32[3,17,270]{2,1,0:T(8,128)S(1)}, f32[17,270]{1,0:T(8,128)}, f32[17,270]{1,0:T(8,128)}, f32[3,17,150]{2,1,0:T(8,128)S(1)}, /*index=5*/f32[3,17,150]{2,1,0:T(8,128)S(1)}) custom-call(f32[680,128]{1,0:T(8,128)S(1)} %get-tuple-element.28.refs_0_, f32[17,8,128]{2,1,0:T(8,128)S(1)} %get-tuple-element.29.refs_1_, ...), custom_call_target="tpu_custom_call" | custom-call | tf_op jit(solution)/shard_map/pallas_call | solution.py:618
  47.9 0.7 %copy.45 = f32[3,17,270]{2,0,1:T(4,128)} copy(f32[3,17,270]{2,1,0:T(8,128)S(1)} %get-tuple-element.46) | data formatting | bytes 110160
  48.6 0.7 %copy.48 = f32[3,17,150]{2,0,1:T(4,128)} copy(f32[3,17,150]{2,1,0:T(8,128)S(1)} %get-tuple-element.52) | data formatting | bytes 61200
  49.2 0.7 %copy.49 = f32[3,17,150]{2,0,1:T(4,128)} copy(f32[3,17,150]{2,1,0:T(8,128)S(1)} %get-tuple-element.53) | data formatting | bytes 61200
  49.9 0.7 %copy.46 = f32[3,17,270]{2,0,1:T(4,128)} copy(f32[3,17,270]{2,1,0:T(8,128)S(1)} %get-tuple-element.47) | data formatting | bytes 110160
  (10 shorter events, 0.1 us)
Async XLA Ops:
  0.6 0.9 %copy-start.14 = (f32[3,17,150]{2,0,1:T(4,128)S(1)}, f32[3,17,150]{2,0,1:T(4,128)}, u32[]{:S(2)}) copy-start(f32[3,17,150]{2,0,1:T(4,128)} %param.33) | copy-start | bytes 91804
  1.5 0.9 %copy-start.15 = (f32[3,17,150]{2,0,1:T(4,128)S(1)}, f32[3,17,150]{2,0,1:T(4,128)}, u32[]{:S(2)}) copy-start(f32[3,17,150]{2,0,1:T(4,128)} %param.34) | copy-start | bytes 91804
  2.4 0.8 %copy-start.18 = (f32[2,17,270]{2,0,1:T(2,128)S(1)}, f32[2,17,270]{2,0,1:T(2,128)}, u32[]{:S(2)}) copy-start(f32[2,17,270]{2,0,1:T(2,128)} %param.24) | copy-start | bytes 110164
  3.2 0.9 %copy-start.16 = (f32[3,17,150]{2,0,1:T(4,128)S(1)}, f32[3,17,150]{2,0,1:T(4,128)}, u32[]{:S(2)}) copy-start(f32[3,17,150]{2,0,1:T(4,128)} %param.32) | copy-start | bytes 91804
  4.1 0.9 %copy-start.17 = (f32[3,17,150]{2,0,1:T(4,128)S(1)}, f32[3,17,150]{2,0,1:T(4,128)}, u32[]{:S(2)}) copy-start(f32[3,17,150]{2,0,1:T(4,128)} %param.35) | copy-start | bytes 91804
  5.0 0.9 %copy-start.9 = (f32[3,17,270]{2,0,1:T(4,128)S(1)}, f32[3,17,270]{2,0,1:T(4,128)}, u32[]{:S(2)}) copy-start(f32[3,17,270]{2,0,1:T(4,128)} %param.21) | copy-start | bytes 165244
  5.9 0.9 %copy-start.10 = (f32[3,17,270]{2,0,1:T(4,128)S(1)}, f32[3,17,270]{2,0,1:T(4,128)}, u32[]{:S(2)}) copy-start(f32[3,17,270]{2,0,1:T(4,128)} %param.22) | copy-start | bytes 165244
  5.9 1.9 %copy-start.13 = (f32[3,17,270]{2,0,1:T(4,128)S(1)}, f32[3,17,270]{2,0,1:T(4,128)}, u32[]{:S(2)}) copy-start(f32[3,17,270]{2,0,1:T(4,128)} %param.29) | copy-start | bytes 165244
  6.8 0.9 %copy-start.11 = (f32[3,17,270]{2,0,1:T(4,128)S(1)}, f32[3,17,270]{2,0,1:T(4,128)}, u32[]{:S(2)}) copy-start(f32[3,17,270]{2,0,1:T(4,128)} %param.20) | copy-start | bytes 165244
  6.8 0.9 %copy-start.12 = (f32[3,17,270]{2,0,1:T(4,128)S(1)}, f32[3,17,270]{2,0,1:T(4,128)}, u32[]{:S(2)}) copy-start(f32[3,17,270]{2,0,1:T(4,128)} %param.23) | copy-start | bytes 165244
  7.7 1.0 %copy-start = (f32[24,24,128]{2,1,0:T(8,128)S(1)}, f32[24,24,128]{2,1,0:T(8,128)}, u32[]{:S(2)}) copy-start(f32[24,24,128]{2,1,0:T(8,128)} %constant.4.clone.refs_18_) | copy-start | bytes 884740
  7.7 0.9 %copy-start.6 = (f32[17,270]{1,0:T(8,128)S(1)}, f32[17,270]{1,0:T(8,128)}, u32[]{:S(2)}) copy-start(f32[17,270]{1,0:T(8,128)} %refs_11_.2) | copy-start | bytes 55084
  7.7 0.9 %copy-start.8 = (f32[24,128]{1,0:T(8,128)S(1)}, f32[24,128]{1,0:T(8,128)}, u32[]{:S(2)}) copy-start(f32[24,128]{1,0:T(8,128)} %constant.5.clone.refs_19_) | copy-start | bytes 36868
  7.7 0.9 %copy-start.1 = (f32[17,270]{1,0:T(8,128)S(1)}, f32[17,270]{1,0:T(8,128)}, u32[]{:S(2)}) copy-start(f32[17,270]{1,0:T(8,128)} %refs_11_.3) | copy-start | bytes 55084
  7.8 0.9 %copy-start.2 = (f32[17,270]{1,0:T(8,128)S(1)}, f32[17,270]{1,0:T(8,128)}, u32[]{:S(2)}) copy-start(f32[17,270]{1,0:T(8,128)} %refs_12_.2) | copy-start | bytes 55084
  7.8 0.9 %copy-start.3 = (f32[17,270]{1,0:T(8,128)S(1)}, f32[17,270]{1,0:T(8,128)}, u32[]{:S(2)}) copy-start(f32[17,270]{1,0:T(8,128)} %refs_5_.1) | copy-start | bytes 55084
  7.8 0.9 %copy-start.4 = (f32[17,270]{1,0:T(8,128)S(1)}, f32[17,270]{1,0:T(8,128)}, u32[]{:S(2)}) copy-start(f32[17,270]{1,0:T(8,128)} %refs_6_.1) | copy-start | bytes 55084
  7.8 0.9 %copy-start.5 = (f32[17,270]{1,0:T(8,128)S(1)}, f32[17,270]{1,0:T(8,128)}, u32[]{:S(2)}) copy-start(f32[17,270]{1,0:T(8,128)} %refs_10_.2) | copy-start | bytes 55084
  7.8 0.9 %copy-start.7 = (f32[17,150]{1,0:T(8,128)S(1)}, f32[17,150]{1,0:T(8,128)}, u32[]{:S(2)}) copy-start(f32[17,150]{1,0:T(8,128)} %refs_17_.1) | copy-start | bytes 30604

commit v2 on v1

--- a/solution.py
+++ b/solution.py
@@ -134,9 +134,9 @@
     return pad[...]
 
 
-def local_phase(ins, disp_outs, store_tile, scratch):
+def local_phase(ins, keep, store_tile, scratch, ready):
     (md, mv, ma, mg, mm, mr, cp, cr, ca, cg, ck, crho, nd, nv, na, ng, nm, nr, row_table, lane_table) = ins
-    md_new, cp_new, nd_new = disp_outs
+    md_new, cp_new, nd_new, mv_half, cr_half, nv_half = keep
     wide, narrow = scratch
 
     def rows(index):
@@ -148,16 +148,22 @@
     wide[...] = jnp.ones_like(wide)
     narrow[...] = jnp.ones_like(narrow)
     displace = []
+    ready(range(6))
     for i in range(3):
-        outer = md[i] + STEP * mv[i] + HALF_SQUARE * ma[i]
-        inner = nd[i] + STEP * nv[i] + HALF_SQUARE * na[i]
-        md_new[i] = outer
-        nd_new[i] = inner
+        outer = md[:, i, :] + STEP * mv[:, i, :] + HALF_SQUARE * ma[:, i, :]
+        inner = nd[:, i, :] + STEP * nv[:, i, :] + HALF_SQUARE * na[:, i, :]
+        md_new[:, i, :] = outer
+        nd_new[:, i, :] = inner
         displace.append(slabs(widen(wide, outer), widen(narrow, inner), 0.0))
+    ready(range(6, 20))
+    for i in range(3):
+        mv_half[:, i, :] = mv[:, i, :] + HALF_STEP * ma[:, i, :]
+        nv_half[:, i, :] = nv[:, i, :] + HALF_STEP * na[:, i, :]
+    cr_half[...] = cr[...] + HALF_STEP * ca[...]
     row = lax.broadcasted_iota(jnp.int32, (PAD, LANES), 0)
     displace = [jnp.where((row < ROWS)[None], u, 0.0) for u in displace]
-    scale = [slabs(widen(wide, mg[i]), widen(narrow, ng[i]), 1.0) for i in range(3)]
-    lam, mu = [slabs(widen(wide, mm[i]), widen(narrow, nm[i]), 1.0) for i in range(2)]
+    scale = [slabs(widen(wide, mg[:, i, :]), widen(narrow, ng[:, i, :]), 1.0) for i in range(3)]
+    lam, mu = [slabs(widen(wide, mm[:, i, :]), widen(narrow, nm[:, i, :]), 1.0) for i in range(2)]
     density = slabs(widen(wide, mr[...]), widen(narrow, nr[...]), 1.0)
     row_column = jnp.stack([row_table[LUMPED] * float(WEIGHTS[x]) for x in range(5)])
     weight = row_column * lanes(LUMPED)
@@ -191,7 +197,7 @@
     outer = cp[...] + STEP * cr[...] + HALF_SQUARE * ca[...]
     cp_new[...] = outer
     potential = jnp.where((row < ROWS)[None], slabs(widen(wide, outer), None, 0.0), 0.0)
-    scale = [slabs(widen(wide, cg[i]), None, 1.0) for i in range(3)]
+    scale = [slabs(widen(wide, cg[:, i, :]), None, 1.0) for i in range(3)]
     kappa = slabs(widen(wide, ck[...]), None, 1.0)
     density = slabs(widen(wide, crho[...]), None, 1.0)
     face = row_column / (scale[0] * scale[1])
@@ -439,14 +445,11 @@
     masks = group_masks((8, LANES))
     big_masks = group_masks((17, 8, LANES))
 
-    def span(x, y):
-        return pl.ds(8 * (17 * x + y), 8)
-
     def add(x, y, values):
-        work[span(x, y), :] += values
+        work[x, y] += values
 
     def add_column(x, values):
-        work[pl.ds(8 * 17 * x, 8 * 17), :] += values.reshape(8 * 17, LANES)
+        work[x] += values
 
     @pl.when(I != 0)
     def _():
@@ -521,7 +524,7 @@
 
 
 def output_phase(load_tile, ins, outs):
-    mv, ma, cr, ca, nv, na = ins
+    mv_half, cr_half, nv_half = ins
     mv_new, ma_new, cr_new, ca_new, nv_new, na_new = outs
     lane = lane_index((1, ROWS, LANES))
     core = load_tile(4)
@@ -545,84 +548,108 @@
     for i in range(3):
         new = (force if i == 2 else load_tile(i)) / mass
         outer = gather(new, 0, 54, 384)[:, :270]
-        ma_new[i] = outer
-        mv_new[i] = mv[i] + HALF_STEP * (ma[i] + outer)
+        ma_new[:, i, :] = outer
+        mv_new[:, i, :] = mv_half[:, i, :] + HALF_STEP * outer
         inner = gather(new, 54, 30, 256)[:, :150]
-        na_new[i] = inner
-        nv_new[i] = nv[i] + HALF_STEP * (na[i] + inner)
+        na_new[:, i, :] = inner
+        nv_new[:, i, :] = nv_half[:, i, :] + HALF_STEP * inner
     outer = gather(accel, 0, 54, 384)[:, :270]
     ca_new[...] = outer
-    cr_new[...] = cr[...] + HALF_STEP * (ca[...] + outer)
-
-
-def local_kernel(*refs):
-    ins, disp_outs, z, scratch = refs[:20], refs[20:23], refs[23], refs[24:]
-    z[...] = jnp.zeros_like(z)
+    cr_new[...] = cr_half[...] + HALF_STEP * outer
+
+
+FETCH = (0, 1, 2, 12, 13, 14, 18, 19, 3, 15, 4, 16, 5, 17, 6, 7, 8, 9, 10, 11)
+
+
+def local_kernel(n_xi, n_eta, *refs):
+    sources, keep, z, bufs = refs[:20], refs[20:26], refs[26], refs[27:35]
+    ins, (wide, narrow, edge_rows, fetch, send, recv) = refs[35:55], refs[55:]
+    fetches = [pltpu.make_async_copy(sources[n], ins[n], fetch.at[n]) for n in FETCH]
+    for item in fetches:
+        item.start()
+
+    def ready(steps):
+        for n in steps:
+            fetches[n].wait()
 
     def store_tile(t, values):
         for x in range(5):
-            z[pl.ds(8 * ROWS * x + t, ROWS, stride=8), :] = values[x, :ROWS]
-
-    local_phase(ins, disp_outs, store_tile, scratch)
-
-
-def exchange_kernel(n_xi, n_eta, z, *refs):
-    bufs, (edge_rows, send, recv) = refs[:8], refs[8:]
-    exchange_phase(n_xi, n_eta, z, bufs + (edge_rows,), (send, recv))
+            z[x, :, t, :] = values[x, :ROWS]
+
+    def work():
+        for t in (6, 7):
+            store_tile(t, jnp.zeros((5, ROWS, LANES), F32))
+        local_phase(ins, keep, store_tile, (wide, narrow), ready)
+
+    exchange_phase(n_xi, n_eta, z, bufs + (edge_rows,), (send, recv), work)
 
 
 def output_kernel(n_xi, n_eta, *refs):
-    z, bufs, ins, outs, work = refs[0], refs[1:9], refs[9:15], refs[15:21], refs[21]
+    z, bufs, kept, halves = refs[0], refs[1:9], refs[9:12], refs[12:15]
+    copies_out, outs, (work, sem) = refs[15:18], refs[18:24], refs[24:]
+    writes = [pltpu.make_async_copy(kept[n], copies_out[n], sem.at[n]) for n in range(3)]
+    for item in writes:
+        item.start()
     work[...] = z[...]
     total_phase(n_xi, n_eta, work, bufs)
 
     def load_tile(t):
-        return jnp.stack([work[pl.ds(8 * ROWS * x + t, ROWS, stride=8), :] for x in range(5)])
-
-    output_phase(load_tile, ins, outs)
+        return jnp.stack([work[x, :, t, :] for x in range(5)])
+
+    output_phase(load_tile, halves, outs)
+    for item in writes:
+        item.wait()
 
 
 def solution(mesh):
     n_xi, n_eta = mesh.shape["xi"], mesh.shape["eta"]
     row_table, lane_table = coefficient_tables()
     vmem = pl.BlockSpec(memory_space=pltpu.VMEM)
+    hbm = pl.BlockSpec(memory_space=pltpu.HBM)
 
     def shape(*dims):
         return jax.ShapeDtypeStruct(dims, F32)
 
-    def step(md, mv, ma, mg, mm, mr, cp, cr, ca, cg, ck, crho, nd, nv, na, ng, nm, nr):
-        ins = (md, mv, ma, mg, mm, mr, cp, cr, ca, cg, ck, crho, nd, nv, na, ng, nm, nr)
-        big, thin, small = shape(*md.shape), shape(*cp.shape), shape(*nd.shape)
-        md_new, cp_new, nd_new, z = pl.pallas_call(
-            local_kernel,
-            out_shape=(big, thin, small, shape(5 * ROWS * 8, LANES)),
-            in_specs=[vmem] * 20,
-            out_specs=[vmem] * 4,
-            scratch_shapes=[pltpu.VMEM((PAD, 384), F32), pltpu.VMEM((PAD, 256), F32)],
-            compiler_params=pltpu.CompilerParams(vmem_limit_bytes=32 * 1024 * 1024),
-        )(*ins, jnp.asarray(row_table), jnp.asarray(lane_table))
-        bufs = pl.pallas_call(
-            functools.partial(exchange_kernel, n_xi, n_eta),
-            out_shape=tuple(shape(*dims) for dims in EXCHANGE_SHAPES),
-            in_specs=[vmem],
-            out_specs=[vmem] * 8,
-            scratch_shapes=[
+    def by_row(values):
+        return jnp.swapaxes(values, 0, 1)
+
+    def step(*arguments):
+        ins = [by_row(a) if a.ndim == 3 else a for a in arguments]
+        ins += [jnp.asarray(row_table), jnp.asarray(lane_table)]
+        ins = [pltpu.with_memory_space_constraint(a, pltpu.HBM) for a in ins]
+        big, thin, small = shape(*ins[0].shape), shape(*ins[6].shape), shape(*ins[12].shape)
+        first = pl.pallas_call(
+            functools.partial(local_kernel, n_xi, n_eta),
+            out_shape=(big, thin, small) * 2
+            + (shape(5, ROWS, 8, LANES),)
+            + tuple(shape(*dims) for dims in EXCHANGE_SHAPES),
+            in_specs=[hbm] * 20,
+            out_specs=[vmem] * 15,
+            scratch_shapes=[pltpu.VMEM(a.shape, F32) for a in ins]
+            + [
+                pltpu.VMEM((PAD, 384), F32),
+                pltpu.VMEM((PAD, 256), F32),
                 pltpu.VMEM(EDGE_SHAPE, F32),
+                pltpu.SemaphoreType.DMA((20,)),
                 pltpu.SemaphoreType.DMA((SENDS,)),
                 pltpu.SemaphoreType.DMA((RECEIVES,)),
             ],
             compiler_params=pltpu.CompilerParams(
                 collective_id=0, has_side_effects=True, vmem_limit_bytes=32 * 1024 * 1024
             ),
-        )(z.reshape(5, ROWS, 8, LANES))
-        mv_new, ma_new, cr_new, ca_new, nv_new, na_new = pl.pallas_call(
+        )(*ins)
+        kept, halves, z, bufs = first[:3], first[3:6], first[6], first[7:]
+        outs = pl.pallas_call(
             functools.partial(output_kernel, n_xi, n_eta),
-            out_shape=(big, big, thin, thin, small, small),
+            out_shape=(big, thin, small) + (big, big, thin, thin, small, small),
             in_specs=[vmem] * 15,
-            out_specs=[vmem] * 6,
-            scratch_shapes=[pltpu.VMEM((5 * ROWS * 8, LANES), F32)],
+            out_specs=[hbm] * 3 + [vmem] * 6,
+            scratch_shapes=[pltpu.VMEM((5, ROWS, 8, LANES), F32), pltpu.SemaphoreType.DMA((3,))],
             compiler_params=pltpu.CompilerParams(vmem_limit_bytes=32 * 1024 * 1024),
-        )(z, *bufs, mv, ma, cr, ca, nv, na)
+        )(z, *bufs, *kept, *halves)
+        md_new, cp_new, nd_new, mv_new, ma_new, cr_new, ca_new, nv_new, na_new = [
+            by_row(a) if a.ndim == 3 else a for a in outs
+        ]
         return md_new, mv_new, ma_new, cp_new, cr_new, ca_new, nd_new, nv_new, na_new
 
     wide, thin = P(None, "eta", "xi"), P("eta", "xi")

time: 51 us -> 36.5 us (0.72)
  the two profiles are of different devices: /device:TPU:2 before, /device:TPU:16 now
where the time goes in v2:
time: 36.5 us; the launch traced here: 36.3 us
  Pallas kernels  35.7 us (98%)
  between operations  0.66 us (2%)
    pallas_call x1, Pallas kernels, step(): pl.pallas_call(functools.partial(local_kernel, n_xi, n_eta), out_shape=(b...  34.1 us
    pallas_call x1, Pallas kernels, step(): pl.pallas_call(functools.partial(output_kernel, n_xi, n_eta), out_shape=(...  1.52 us

profile of v2, /device:TPU:16, one launch (start us, length us, event | category | flops | bytes accessed | tf_op | source)
XLA Modules:
  0.0 36.3 jit_solution(4353771709689702178)
XLA Ops:
  0.6 34.1 %shard_map.259 = (f32[17,3,270]{2,1,0:T(4,128)S(1)}, f32[17,270]{1,0:T(8,128)S(1)}, f32[17,3,150]{2,1,0:T(4,128)S(1)}, f32[17,3,270]{2,1,0:T(4,128)S(1)}, f32[17...) custom-call(f32[17,3,270]{2,1,0:T(4,128)} %bitcast.17, ...), custom_call_target="tpu_custom_call" | custom-call | tf_op jit(solution)/shard_map/pallas_call | solution.py:621
  34.8 1.5 %shard_map.260 = (f32[17,3,270]{2,1,0:T(4,128)}, f32[17,270]{1,0:T(8,128)}, f32[17,3,150]{2,1,0:T(4,128)}, f32[17,3,270]{2,1,0:T(4,128)}, f32[17,3,270]{2,1,0:T(...) custom-call(f32[5,17,8,128]{3,2,1,0:T(8,128)S(1)} %get-tuple-element.33.refs_0_, ...), custom_call_target="tpu_custom_call" | custom-call | tf_op jit(solution)/shard_map/pallas_call | solution.py:642

commit v3 on v2

--- a/solution.py
+++ b/solution.py
@@ -246,12 +246,26 @@
     return result
 
 
+def pack_group(tiles, group, masks):
+    nine, five = masks
+    result = jnp.zeros_like(tiles[0])
+    for i, tile in enumerate(tiles):
+        long, short = turn(tile, 9 * (i - group), 1), turn(tile, 5 * (i - group), 1)
+        result = jnp.where(nine[i], long, jnp.where(five[i], short, result))
+    return result
+
+
 FROM_LEFT = ((3, 0), (0, 1), (1, 2), (2, 3))
 FROM_RIGHT = ((1, 0), (2, 1), (3, 2), (0, 3))
 
 
+SEND_LEFT, SEND_RIGHT, SEND_ROWS, SEND_POLAR, SEND_EXTRA, SENDS = 0, 3, 6, 11, 19, 23
+RECV_LEFT, RECV_RIGHT, RECV_ROWS, RECV_SLOTS, RECV_POLAR, RECV_EXTRA, RECEIVES = 0, 3, 6, 9, 17, 19, 21
+
+
 def exchange_phase(n_xi, n_eta, z, bufs, sems, before_send=None):
-    col_left, col_right, row_below, row_above, mirror, slots, polar, polar_extra, edge_rows = bufs
+    col_left, col_right, row_below, row_above, mirror, slots, polar, polar_extra = bufs[:8]
+    edge_rows, out_sides, out_mirror, out_polar = bufs[8:]
     send, recv = sems
     I, J = lax.axis_index("xi"), lax.axis_index("eta")
     last_i, last_j = n_xi - 1, n_eta - 1
@@ -281,15 +295,20 @@
     def main_copies():
         copies = []
         for q in range(4):
-            src = z.at[4 * far, pl.ds(4 * q, 5)]
             dst = polar.at[1 - far]
-            copies.append((copy(src, dst, 7 + q, 13 + 1 - far, (i_top(q), last_j)), J != last_j if q == 3 else None))
-            copies.append((copy(src, dst, 11 + q, 13 + 1 - far, (i_bottom(q), 0)), J != 0 if q == 0 else None))
-        for q, y, s, exists in ((-1, 0, 15, J != 0), (4, 16, 17, J != last_j)):
+            to_top = copy(out_polar.at[1, q], dst, SEND_POLAR + q, RECV_POLAR + 1 - far, (i_top(q), last_j))
+            to_bottom = copy(out_polar.at[0, q], dst, SEND_POLAR + 4 + q, RECV_POLAR + 1 - far, (i_bottom(q), 0))
+            copies.append((to_top, J != last_j if q == 3 else None))
+            copies.append((to_bottom, J != 0 if q == 0 else None))
+        return copies
+
+    def extra_copies():
+        copies = []
+        for q, y, s, exists in ((-1, 0, SEND_EXTRA, J != 0), (4, 16, SEND_EXTRA + 2, J != last_j)):
             src = z.at[4 * far, y]
             dst = polar_extra.at[1 - far]
-            copies.append((copy(src, dst, s, 15 + 1 - far, (i_top(q), last_j)), exists))
-            copies.append((copy(src, dst, s + 1, 15 + 1 - far, (i_bottom(q), 0)), exists))
+            copies.append((copy(src, dst, s, RECV_EXTRA + 1 - far, (i_top(q), last_j)), exists))
+            copies.append((copy(src, dst, s + 1, RECV_EXTRA + 1 - far, (i_bottom(q), 0)), exists))
         return copies
 
     def guarded(condition, action):
@@ -334,50 +353,77 @@
     partners = 4 + (top + bottom) * (3 - far - near) + (far + near) * (12 - 3 * top - 3 * bottom)
     pl.semaphore_wait(barrier, partners)
 
-    to_left = copy(z.at[0], col_right, 0, 1, (left, J))
-    to_right = copy(z.at[4], col_left, 1, 0, (right, J))
+    corners = []
+    for n, y in enumerate((0, 16)):
+        corners.append(copy(z.at[0, y], col_right.at[y], SEND_LEFT + n, RECV_RIGHT + n, (left, J)))
+        corners.append(copy(z.at[4, y], col_left.at[y], SEND_RIGHT + n, RECV_LEFT + n, (right, J)))
+    inner = pl.ds(1, 15)
+    to_left = copy(z.at[0, inner], col_right.at[inner], SEND_LEFT + 2, RECV_RIGHT + 2, (left, J))
+    to_right = copy(z.at[4, inner], col_left.at[inner], SEND_RIGHT + 2, RECV_LEFT + 2, (right, J))
+    for item in corners:
+        item.start()
+
+    masks = group_masks((8, LANES))
+
+    @pl.when(at_side)
+    def _():
+        for item, condition in extra_copies():
+            guarded(condition, item.start)
+        for q in range(4):
+            rows = [z[4 * far, 4 * q + i] for i in range(5)]
+            out_polar[1, q] = pack_group(rows, 4, masks)
+            out_polar[0, q] = pack_group(rows, 5, masks)
+        for item, condition in main_copies():
+            guarded(condition, item.start)
+        pl.when(J == last_j)(lambda: polar.__setitem__(1 - far, out_polar[1, 3]))
+        pl.when(J == 0)(lambda: polar.__setitem__(1 - far, out_polar[0, 0]))
+
     to_left.start()
     to_right.start()
 
-    @pl.when(at_side)
-    def _():
-        for item, condition in main_copies():
-            guarded(condition, item.start)
-        pl.when(J == last_j)(lambda: polar.__setitem__(1 - far, z[4 * far, pl.ds(12, 5)]))
-        pl.when(J == 0)(lambda: polar.__setitem__(1 - far, z[4 * far, pl.ds(0, 5)]))
-
-    masks = group_masks((8, LANES))
     for end, y in ((0, 0), (1, 16)):
         for x in range(1, 4):
             edge_rows[end, x] = z[x, y]
-    to_right.wait_recv()
+    for item in corners:
+        item.wait_recv()
     for end, y in ((0, 0), (1, 16)):
         got = col_left[y]
         got = jnp.where(I == 0, move_groups(got, FROM_LEFT, masks), got)
         edge_rows[end, 0] = z[0, y] + got
-    to_left.wait_recv()
-    for end, y in ((0, 0), (1, 16)):
         got = col_right[y]
         got = jnp.where(I == last_i, move_groups(got, FROM_RIGHT, masks), got)
         edge_rows[end, 4] = z[4, y] + got
 
-    to_up = copy(edge_rows.at[1], row_below, 2, 2, (I, up))
-    to_down = copy(edge_rows.at[0], row_above, 3, 3, (I, down))
-    to_mirror = copy(edge_rows.at[top], mirror, 4, 4, (last_i - I, J))
+    to_up = copy(edge_rows.at[1], row_below, SEND_ROWS, RECV_ROWS, (I, up))
+    to_down = copy(edge_rows.at[0], row_above, SEND_ROWS + 1, RECV_ROWS + 1, (I, down))
+    to_mirror = copy(out_mirror, mirror, SEND_ROWS + 2, RECV_ROWS + 2, (last_i - I, J))
     slot = slots.at[top, I % 4]
-    to_far = copy(edge_rows.at[top], slot, 5, 5 + 4 * top + I % 4, (last_i, j_right))
-    to_near = copy(edge_rows.at[top], slot, 6, 5 + 4 * top + I % 4, (0, j_left))
+    slot_recv = RECV_SLOTS + 4 * top + I % 4
+    to_far = copy(out_sides.at[0], slot, SEND_ROWS + 3, slot_recv, (last_i, j_right))
+    to_near = copy(out_sides.at[1], slot, SEND_ROWS + 4, slot_recv, (0, j_left))
+    to_up.start()
+    to_down.start()
 
     @pl.when(at_edge)
     def _():
-        to_mirror.start()
+        for end in range(2):
+
+            @pl.when(J == end * last_j)
+            def _():
+                rows = [edge_rows[end, x] for x in range(5)]
+                out_sides[0] = pack_group(rows, 1, masks)
+                out_sides[1] = pack_group(rows, 3, masks)
+                out_mirror[0] = pack_group(rows, 2, masks)
+                out_mirror[1] = pack_group(rows, 4 if end == 1 else 5, masks)
+
         pl.when(I != last_i)(to_far.start)
         pl.when(I != 0)(to_near.start)
-        pl.when(I % last_i == 0)(lambda: slots.__setitem__((top, I % 4), edge_rows[top]))
-
-    to_up.start()
-    to_down.start()
-
+        to_mirror.start()
+        pl.when(I == last_i)(lambda: slots.__setitem__((top, 3), out_sides[0]))
+        pl.when(I == 0)(lambda: slots.__setitem__((top, 0), out_sides[1]))
+
+    to_left.wait_recv()
+    to_right.wait_recv()
     to_up.wait_recv()
     to_down.wait_recv()
 
@@ -385,7 +431,7 @@
     def _():
         to_mirror.wait_recv()
         for k in range(2):
-            main = copy(z.at[0, pl.ds(0, 5)], polar.at[k], 7, 13 + k, (left, J))
+            main = copy(out_polar.at[0, 0], polar.at[k], SEND_POLAR, RECV_POLAR + k, (left, J))
             pl.when(I != (last_i if k == 0 else 0))(main.wait_recv)
 
         @pl.when(has_extra)
@@ -393,19 +439,21 @@
             @pl.when(I % last_i != 0)
             def _():
                 for k in range(2):
-                    copy(z.at[0, 0], polar_extra.at[k], 15, 15 + k, (left, J)).wait_recv()
+                    copy(z.at[0, 0], polar_extra.at[k], SEND_EXTRA, RECV_EXTRA + k, (left, J)).wait_recv()
 
     @pl.when(at_side)
     def _():
         for end in range(2):
             for j in range(4):
-                arrival = copy(edge_rows.at[0], slots.at[end, j], 5, 5 + 4 * end + j, (left, J))
+                arrival = copy(out_sides.at[0], slots.at[end, j], SEND_ROWS + 3, RECV_SLOTS + 4 * end + j, (left, J))
                 if j in (0, 3):
                     away = (J - end * last_j) * (J - end * last_j) + (3 * far - j) * (3 * far - j)
                     pl.when(away != 0)(arrival.wait_recv)
                 else:
                     arrival.wait_recv()
 
+    for item in corners:
+        item.wait_send()
     to_left.wait_send()
     to_right.wait_send()
     to_up.wait_send()
@@ -419,7 +467,7 @@
 
     @pl.when(at_side)
     def _():
-        for item, condition in main_copies():
+        for item, condition in main_copies() + extra_copies():
             guarded(condition, item.wait_send)
 
 
@@ -428,13 +476,12 @@
     (17, 8, LANES),
     (5, 8, LANES),
     (5, 8, LANES),
-    (5, 8, LANES),
-    (2, 4, 5, 8, LANES),
-    (2, 5, 8, LANES),
+    (2, 8, LANES),
+    (2, 4, 8, LANES),
+    (2, 8, LANES),
     (2, 8, LANES),
 )
-EDGE_SHAPE = (2, 5, 8, LANES)
-SENDS, RECEIVES = 19, 17
+OUT_SHAPES = ((2, 5, 8, LANES), (2, 8, LANES), (2, 8, LANES), (2, 4, 8, LANES))
 
 
 def total_phase(n_xi, n_eta, work, bufs):
@@ -486,9 +533,10 @@
         def _():
             for x in range(5):
                 value = move_groups(ring[x], ring_pairs, masks)
-                value = value + move_groups(mirror[4 - x], ((2, pole), (pole, 2)), masks)
-                value = value + move_groups(polar[0, x if end == 1 else 4 - x], ((pole, 1),), masks)
-                value = value + move_groups(polar[1, 4 - x if end == 1 else x], ((pole, 3),), masks)
+                value = value + move_groups(mirror[0], ((4 - x, pole),), masks)
+                value = value + move_groups(mirror[1], ((4 - x, 2),), masks)
+                value = value + move_groups(polar[0], ((x if end == 1 else 4 - x, 1),), masks)
+                value = value + move_groups(polar[1], ((4 - x if end == 1 else x, 3),), masks)
                 add(x, y, value)
 
             def extra(x):
@@ -513,7 +561,7 @@
                     j, x = min(point // 4, 3), point - 4 * min(point // 4, 3)
 
                     def place(y=y, j=j, x=x):
-                        add(4 * side, y, move_groups(slots[end, j, x], ((group, pole),), masks))
+                        add(4 * side, y, move_groups(slots[end, j], ((x, pole),), masks))
 
                     if y == 0:
                         pl.when(J != 0)(place)
@@ -563,7 +611,7 @@
 
 def local_kernel(n_xi, n_eta, *refs):
     sources, keep, z, bufs = refs[:20], refs[20:26], refs[26], refs[27:35]
-    ins, (wide, narrow, edge_rows, fetch, send, recv) = refs[35:55], refs[55:]
+    ins, (wide, narrow), outgoing, (fetch, send, recv) = refs[35:55], refs[55:57], refs[57:61], refs[61:]
     fetches = [pltpu.make_async_copy(sources[n], ins[n], fetch.at[n]) for n in FETCH]
     for item in fetches:
         item.start()
@@ -581,7 +629,7 @@
             store_tile(t, jnp.zeros((5, ROWS, LANES), F32))
         local_phase(ins, keep, store_tile, (wide, narrow), ready)
 
-    exchange_phase(n_xi, n_eta, z, bufs + (edge_rows,), (send, recv), work)
+    exchange_phase(n_xi, n_eta, z, bufs + outgoing, (send, recv), work)
 
 
 def output_kernel(n_xi, n_eta, *refs):
@@ -629,7 +677,9 @@
             + [
                 pltpu.VMEM((PAD, 384), F32),
                 pltpu.VMEM((PAD, 256), F32),
-                pltpu.VMEM(EDGE_SHAPE, F32),
+            ]
+            + [pltpu.VMEM(dims, F32) for dims in OUT_SHAPES]
+            + [
                 pltpu.SemaphoreType.DMA((20,)),
                 pltpu.SemaphoreType.DMA((SENDS,)),
                 pltpu.SemaphoreType.DMA((RECEIVES,)),

time: 36.5 us -> 35.7 us (0.978)
  the two profiles are of different devices: /device:TPU:16 before, /device:TPU:2 now
where the time goes in v3:
time: 35.7 us; the launch traced here: 35.5 us
  Pallas kernels  34.9 us (98%)
  between operations  0.66 us (2%)
    pallas_call x1, Pallas kernels, step(): pl.pallas_call(functools.partial(local_kernel, n_xi, n_eta), out_shape=(b...  33 us
    pallas_call x1, Pallas kernels, step(): pl.pallas_call(functools.partial(output_kernel, n_xi, n_eta), out_shape=(...  1.84 us

profile of v3, /device:TPU:2, one launch (start us, length us, event | category | flops | bytes accessed | tf_op | source)
XLA Modules:
  0.0 35.5 jit_solution(3097521397271545663)
XLA Ops:
  0.6 33.0 %shard_map.259 = (f32[17,3,270]{2,1,0:T(4,128)S(1)}, f32[17,270]{1,0:T(8,128)S(1)}, f32[17,3,150]{2,1,0:T(4,128)S(1)}, f32[17,3,270]{2,1,0:T(4,128)S(1)}, f32[17...) custom-call(f32[17,3,270]{2,1,0:T(4,128)} %bitcast.17, ...), custom_call_target="tpu_custom_call" | custom-call | tf_op jit(solution)/shard_map/pallas_call | solution.py:669
  33.7 1.8 %shard_map.260 = (f32[17,3,270]{2,1,0:T(4,128)}, f32[17,270]{1,0:T(8,128)}, f32[17,3,150]{2,1,0:T(4,128)}, f32[17,3,270]{2,1,0:T(4,128)}, f32[17,3,270]{2,1,0:T(...) custom-call(f32[5,17,8,128]{3,2,1,0:T(8,128)S(1)} %get-tuple-element.33.refs_0_, ...), custom_call_target="tpu_custom_call" | custom-call | tf_op jit(solution)/shard_map/pallas_call | solution.py:692

commit v4 on v3

--- a/solution.py
+++ b/solution.py
@@ -259,27 +259,35 @@
 FROM_RIGHT = ((1, 0), (2, 1), (3, 2), (0, 3))
 
 
-SEND_LEFT, SEND_RIGHT, SEND_ROWS, SEND_POLAR, SEND_EXTRA, SENDS = 0, 3, 6, 11, 19, 23
-RECV_LEFT, RECV_RIGHT, RECV_ROWS, RECV_SLOTS, RECV_POLAR, RECV_EXTRA, RECEIVES = 0, 3, 6, 9, 17, 19, 21
-
-
-def exchange_phase(n_xi, n_eta, z, bufs, sems, before_send=None):
-    col_left, col_right, row_below, row_above, mirror, slots, polar, polar_extra = bufs[:8]
-    edge_rows, out_sides, out_mirror, out_polar = bufs[8:]
+SEND_COLUMNS, SEND_ROWS, SEND_DIAGONALS, SEND_MIRROR, SEND_SIDES = 0, 2, 4, 8, 11
+SEND_BEYOND, SEND_POLAR, SEND_EXTRA, SENDS = 13, 15, 23, 27
+RECV_COLUMNS, RECV_ROWS, RECV_DIAGONALS, RECV_MIRROR, RECV_SLOTS = 0, 2, 4, 8, 11
+RECV_BEYOND, RECV_POLAR, RECV_EXTRA, RECEIVES = 19, 23, 25, 27
+
+
+def exchange_phase(n_xi, n_eta, z, bufs, sems, before_send):
+    col_left, col_right, row_below, row_above, diagonal, mirror, mirror_ends, slots, beyond, polar, polar_extra = bufs[:11]
+    out_sides, out_mirror, out_polar = bufs[11:]
     send, recv = sems
     I, J = lax.axis_index("xi"), lax.axis_index("eta")
     last_i, last_j = n_xi - 1, n_eta - 1
+    half = n_xi // 2
     left, right = lax.rem(I + n_xi - 1, n_xi), lax.rem(I + 1, n_xi)
     down, up = lax.rem(J + n_eta - 1, n_eta), lax.rem(J + 1, n_eta)
-    top = J // last_j
-    far = I // last_i
+    before_mirror, after_mirror = lax.rem(2 * n_xi - 2 - I, n_xi), lax.rem(n_xi - I, n_xi)
+    top, bottom = J // last_j, (last_j - J) // last_j
+    far, near = I // last_i, (last_i - I) // last_i
     quarter = I // 4
     j_right = top * quarter + (1 - top) * (last_j - quarter)
     j_left = (1 - top) * quarter + top * (last_j - quarter)
-    lean = (2 * ((I % 4) // 3) - 1) * (2 * top - 1)
+    end_x = (I % 4) // 3
+    lean = (2 * end_x - 1) * (2 * top - 1)
     at_edge = J % last_j == 0
     at_side = I % last_i == 0
-    has_extra = ((I + 1) % 4) // 2 == 0
+    extra = 1 - ((I + 1) % 4) // 2
+    has_extra = extra == 1
+    no_turn_after = (I + 1) % half != 0
+    no_turn_before = I % half != 0
 
     def i_top(q):
         return far * (4 * J + q) + (1 - far) * (last_i - 4 * J - q)
@@ -291,6 +299,78 @@
         return pltpu.make_async_remote_copy(
             src_ref=src, dst_ref=dst, send_sem=send.at[s], recv_sem=recv.at[r], device_id=device, device_id_type=MESH
         )
+
+    def guarded(condition, action):
+        if condition is None:
+            action()
+        else:
+            pl.when(condition)(action)
+
+    barrier = pltpu.get_barrier_semaphore()
+
+    def greet(i, j):
+        pl.semaphore_signal(barrier, inc=1, device_id=(i, j), device_id_type=MESH)
+
+    @pl.when(at_edge)
+    def _():
+        greet(last_i - I, J)
+        pl.when(no_turn_after)(lambda: greet(before_mirror, J))
+        pl.when(no_turn_before)(lambda: greet(after_mirror, J))
+        pl.when(I != last_i)(lambda: greet(last_i, j_right))
+        pl.when(I != 0)(lambda: greet(0, j_left))
+
+        @pl.when(has_extra)
+        def _():
+            @pl.when(I % last_i != 0)
+            def _():
+                greet(last_i, j_right + lean)
+                greet(0, j_left - lean)
+
+    @pl.when(at_side)
+    def _():
+        for q in range(4):
+            guarded(J != last_j if q == 3 else None, functools.partial(greet, i_top(q), last_j))
+            guarded(J != 0 if q == 0 else None, functools.partial(greet, i_bottom(q), 0))
+        for q, exists in ((-1, J != 0), (4, J != last_j)):
+            guarded(exists, functools.partial(greet, i_top(q), last_j))
+            guarded(exists, functools.partial(greet, i_bottom(q), 0))
+
+    for i in (left, I, right):
+        for j in (down, J, up):
+            if not (i is I and j is J):
+                greet(i, j)
+
+    before_send()
+
+    turned_after = (I + 1) // half - I // half
+    turned_before = (I + n_xi) // half - (I + n_xi - 1) // half
+    edge_partners = 5 - turned_after - turned_before - far - near + 2 * (extra - far - near)
+    side_partners = 12 - 3 * top - 3 * bottom
+    pl.semaphore_wait(barrier, 8 + (top + bottom) * edge_partners + (far + near) * side_partners)
+
+    base = [
+        copy(z.at[0, 16], diagonal.at[1], SEND_DIAGONALS, RECV_DIAGONALS + 1, (left, up)),
+        copy(z.at[4, 16], diagonal.at[0], SEND_DIAGONALS + 1, RECV_DIAGONALS, (right, up)),
+        copy(z.at[0, 0], diagonal.at[3], SEND_DIAGONALS + 2, RECV_DIAGONALS + 3, (left, down)),
+        copy(z.at[4, 0], diagonal.at[2], SEND_DIAGONALS + 3, RECV_DIAGONALS + 2, (right, down)),
+        copy(z.at[:, 16], row_below, SEND_ROWS, RECV_ROWS, (I, up)),
+        copy(z.at[:, 0], row_above, SEND_ROWS + 1, RECV_ROWS + 1, (I, down)),
+        copy(z.at[0], col_right, SEND_COLUMNS, RECV_COLUMNS + 1, (left, J)),
+        copy(z.at[4], col_left, SEND_COLUMNS + 1, RECV_COLUMNS, (right, J)),
+    ]
+    y_end = 16 * top
+    slot = slots.at[top, I % 4]
+    slot_recv = RECV_SLOTS + 4 * top + I % 4
+    beyond_far, beyond_near = (1 - lean) // 2, (1 + lean) // 2
+    to_mirror = copy(out_mirror, mirror, SEND_MIRROR, RECV_MIRROR, (last_i - I, J))
+    to_before = copy(z.at[4, y_end], mirror_ends.at[0], SEND_MIRROR + 1, RECV_MIRROR + 1, (before_mirror, J))
+    to_after = copy(z.at[0, y_end], mirror_ends.at[1], SEND_MIRROR + 2, RECV_MIRROR + 2, (after_mirror, J))
+    to_far = copy(out_sides.at[0], slot, SEND_SIDES, slot_recv, (last_i, j_right))
+    to_near = copy(out_sides.at[1], slot, SEND_SIDES + 1, slot_recv, (0, j_left))
+    outer = z.at[4 * end_x, y_end]
+    recv_far, recv_near = RECV_BEYOND + 2 * top + beyond_far, RECV_BEYOND + 2 * top + beyond_near
+    past_far = copy(outer, beyond.at[top, beyond_far], SEND_BEYOND, recv_far, (last_i, j_right + lean))
+    past_near = copy(outer, beyond.at[top, beyond_near], SEND_BEYOND + 1, recv_near, (0, j_left - lean))
 
     def main_copies():
         copies = []
@@ -311,59 +391,33 @@
             copies.append((copy(src, dst, s + 1, RECV_EXTRA + 1 - far, (i_bottom(q), 0)), exists))
         return copies
 
-    def guarded(condition, action):
-        if condition is None:
-            action()
-        else:
-            pl.when(condition)(action)
-
-    barrier = pltpu.get_barrier_semaphore()
-
-    def greet(i, j):
-        pl.semaphore_signal(barrier, inc=1, device_id=(i, j), device_id_type=MESH)
-
-    greet(left, J)
-    greet(right, J)
-    greet(I, down)
-    greet(I, up)
+    masks = group_masks((8, LANES))
 
     @pl.when(at_edge)
     def _():
-        greet(last_i - I, J)
-        pl.when(I != last_i)(lambda: greet(last_i, j_right))
-        pl.when(I != 0)(lambda: greet(0, j_left))
+        pl.when(no_turn_after)(to_before.start)
+        pl.when(no_turn_before)(to_after.start)
 
         @pl.when(has_extra)
         def _():
             @pl.when(I % last_i != 0)
             def _():
-                greet(last_i, j_right + lean)
-                greet(0, j_left - lean)
-
-    @pl.when(at_side)
-    def _():
-        for q in range(4):
-            guarded(J != last_j if q == 3 else None, functools.partial(greet, i_top(q), last_j))
-            guarded(J != 0 if q == 0 else None, functools.partial(greet, i_bottom(q), 0))
-
-    if before_send is not None:
-        before_send()
-
-    bottom, near = (last_j - J) // last_j, (last_i - I) // last_i
-    partners = 4 + (top + bottom) * (3 - far - near) + (far + near) * (12 - 3 * top - 3 * bottom)
-    pl.semaphore_wait(barrier, partners)
-
-    corners = []
-    for n, y in enumerate((0, 16)):
-        corners.append(copy(z.at[0, y], col_right.at[y], SEND_LEFT + n, RECV_RIGHT + n, (left, J)))
-        corners.append(copy(z.at[4, y], col_left.at[y], SEND_RIGHT + n, RECV_LEFT + n, (right, J)))
-    inner = pl.ds(1, 15)
-    to_left = copy(z.at[0, inner], col_right.at[inner], SEND_LEFT + 2, RECV_RIGHT + 2, (left, J))
-    to_right = copy(z.at[4, inner], col_left.at[inner], SEND_RIGHT + 2, RECV_LEFT + 2, (right, J))
-    for item in corners:
-        item.start()
-
-    masks = group_masks((8, LANES))
+                past_far.start()
+                past_near.start()
+
+        for end in range(2):
+
+            @pl.when(J == end * last_j)
+            def _():
+                rows = [z[x, 16 * end] for x in range(5)]
+                out_sides[0] = pack_group(rows, 1, masks)
+                out_sides[1] = pack_group(rows, 3, masks)
+                out_mirror[0] = pack_group(rows, 2, masks)
+                out_mirror[1] = pack_group(rows, 4 if end == 1 else 5, masks)
+
+        pl.when(I != last_i)(to_far.start)
+        pl.when(I != 0)(to_near.start)
+        to_mirror.start()
 
     @pl.when(at_side)
     def _():
@@ -375,61 +429,30 @@
             out_polar[0, q] = pack_group(rows, 5, masks)
         for item, condition in main_copies():
             guarded(condition, item.start)
+
+    for item in base:
+        item.start()
+
+    @pl.when(at_edge)
+    def _():
+        pl.when((I + 1) % half == 0)(lambda: mirror_ends.__setitem__(0, z[4, y_end]))
+        pl.when(I % half == 0)(lambda: mirror_ends.__setitem__(1, z[0, y_end]))
+        pl.when(I == last_i)(lambda: slots.__setitem__((top, 3), out_sides[0]))
+        pl.when(I == 0)(lambda: slots.__setitem__((top, 0), out_sides[1]))
+
+    @pl.when(at_side)
+    def _():
         pl.when(J == last_j)(lambda: polar.__setitem__(1 - far, out_polar[1, 3]))
         pl.when(J == 0)(lambda: polar.__setitem__(1 - far, out_polar[0, 0]))
 
-    to_left.start()
-    to_right.start()
-
-    for end, y in ((0, 0), (1, 16)):
-        for x in range(1, 4):
-            edge_rows[end, x] = z[x, y]
-    for item in corners:
+    for item in base:
         item.wait_recv()
-    for end, y in ((0, 0), (1, 16)):
-        got = col_left[y]
-        got = jnp.where(I == 0, move_groups(got, FROM_LEFT, masks), got)
-        edge_rows[end, 0] = z[0, y] + got
-        got = col_right[y]
-        got = jnp.where(I == last_i, move_groups(got, FROM_RIGHT, masks), got)
-        edge_rows[end, 4] = z[4, y] + got
-
-    to_up = copy(edge_rows.at[1], row_below, SEND_ROWS, RECV_ROWS, (I, up))
-    to_down = copy(edge_rows.at[0], row_above, SEND_ROWS + 1, RECV_ROWS + 1, (I, down))
-    to_mirror = copy(out_mirror, mirror, SEND_ROWS + 2, RECV_ROWS + 2, (last_i - I, J))
-    slot = slots.at[top, I % 4]
-    slot_recv = RECV_SLOTS + 4 * top + I % 4
-    to_far = copy(out_sides.at[0], slot, SEND_ROWS + 3, slot_recv, (last_i, j_right))
-    to_near = copy(out_sides.at[1], slot, SEND_ROWS + 4, slot_recv, (0, j_left))
-    to_up.start()
-    to_down.start()
 
     @pl.when(at_edge)
     def _():
-        for end in range(2):
-
-            @pl.when(J == end * last_j)
-            def _():
-                rows = [edge_rows[end, x] for x in range(5)]
-                out_sides[0] = pack_group(rows, 1, masks)
-                out_sides[1] = pack_group(rows, 3, masks)
-                out_mirror[0] = pack_group(rows, 2, masks)
-                out_mirror[1] = pack_group(rows, 4 if end == 1 else 5, masks)
-
-        pl.when(I != last_i)(to_far.start)
-        pl.when(I != 0)(to_near.start)
-        to_mirror.start()
-        pl.when(I == last_i)(lambda: slots.__setitem__((top, 3), out_sides[0]))
-        pl.when(I == 0)(lambda: slots.__setitem__((top, 0), out_sides[1]))
-
-    to_left.wait_recv()
-    to_right.wait_recv()
-    to_up.wait_recv()
-    to_down.wait_recv()
-
-    @pl.when(at_edge)
-    def _():
         to_mirror.wait_recv()
+        pl.when(no_turn_after)(to_before.wait_recv)
+        pl.when(no_turn_before)(to_after.wait_recv)
         for k in range(2):
             main = copy(out_polar.at[0, 0], polar.at[k], SEND_POLAR, RECV_POLAR + k, (left, J))
             pl.when(I != (last_i if k == 0 else 0))(main.wait_recv)
@@ -445,25 +468,33 @@
     def _():
         for end in range(2):
             for j in range(4):
-                arrival = copy(out_sides.at[0], slots.at[end, j], SEND_ROWS + 3, RECV_SLOTS + 4 * end + j, (left, J))
+                arrival = copy(out_sides.at[0], slots.at[end, j], SEND_SIDES, RECV_SLOTS + 4 * end + j, (left, J))
                 if j in (0, 3):
                     away = (J - end * last_j) * (J - end * last_j) + (3 * far - j) * (3 * far - j)
                     pl.when(away != 0)(arrival.wait_recv)
                 else:
                     arrival.wait_recv()
-
-    for item in corners:
+            for n, exists in ((0, J != 0), (1, J != last_j)):
+                arrival = copy(z.at[0, 0], beyond.at[end, n], SEND_BEYOND, RECV_BEYOND + 2 * end + n, (left, J))
+                pl.when(exists)(arrival.wait_recv)
+
+    for item in base:
         item.wait_send()
-    to_left.wait_send()
-    to_right.wait_send()
-    to_up.wait_send()
-    to_down.wait_send()
 
     @pl.when(at_edge)
     def _():
         to_mirror.wait_send()
+        pl.when(no_turn_after)(to_before.wait_send)
+        pl.when(no_turn_before)(to_after.wait_send)
         pl.when(I != last_i)(to_far.wait_send)
         pl.when(I != 0)(to_near.wait_send)
+
+        @pl.when(has_extra)
+        def _():
+            @pl.when(I % last_i != 0)
+            def _():
+                past_far.wait_send()
+                past_near.wait_send()
 
     @pl.when(at_side)
     def _():
@@ -476,67 +507,86 @@
     (17, 8, LANES),
     (5, 8, LANES),
     (5, 8, LANES),
+    (4, 8, LANES),
+    (2, 8, LANES),
     (2, 8, LANES),
     (2, 4, 8, LANES),
+    (2, 2, 8, LANES),
     (2, 8, LANES),
     (2, 8, LANES),
 )
-OUT_SHAPES = ((2, 5, 8, LANES), (2, 8, LANES), (2, 8, LANES), (2, 4, 8, LANES))
+OUT_SHAPES = ((2, 8, LANES), (2, 8, LANES), (2, 4, 8, LANES))
 
 
 def total_phase(n_xi, n_eta, work, bufs):
-    col_left, col_right, row_below, row_above, mirror, slots, polar, polar_extra = bufs
+    col_left, col_right, row_below, row_above, diagonal, mirror, mirror_ends, slots, beyond, polar, polar_extra = bufs
     I, J = lax.axis_index("xi"), lax.axis_index("eta")
     last_i, last_j = n_xi - 1, n_eta - 1
-    far = I // last_i
     masks = group_masks((8, LANES))
     big_masks = group_masks((17, 8, LANES))
 
     def add(x, y, values):
         work[x, y] += values
 
-    def add_column(x, values):
-        work[x] += values
+    def from_left(values, first):
+        return jnp.where(first, move_groups(values, FROM_LEFT, masks), values)
+
+    def from_right(values, last):
+        return jnp.where(last, move_groups(values, FROM_RIGHT, masks), values)
+
+    def completed(row, left_end, right_end):
+        ends = from_left(diagonal[left_end], I == 0), from_right(diagonal[right_end], I == last_i)
+        return [row[0] + ends[0], row[1], row[2], row[3], row[4] + ends[1]]
+
+    below = completed(row_below, 0, 1)
+    above = completed(row_above, 2, 3)
 
     @pl.when(I != 0)
     def _():
-        add_column(0, col_left[...])
+        work[0] += col_left[...]
 
     @pl.when(I != last_i)
     def _():
-        add_column(4, col_right[...])
+        work[4] += col_right[...]
 
     @pl.when(I == 0)
     def _():
-        add_column(0, move_groups(col_left[...], FROM_LEFT, big_masks))
+        work[0] += move_groups(col_left[...], FROM_LEFT, big_masks)
 
     @pl.when(I == last_i)
     def _():
-        add_column(4, move_groups(col_right[...], FROM_RIGHT, big_masks))
+        work[4] += move_groups(col_right[...], FROM_RIGHT, big_masks)
 
     @pl.when(J != last_j)
     def _():
         for x in range(5):
-            add(x, 16, row_above[x])
+            add(x, 16, above[x])
 
     @pl.when(J != 0)
     def _():
         for x in range(5):
-            add(x, 0, row_below[x])
+            add(x, 0, below[x])
 
     for end, y, pole, ring, ring_pairs in (
-        (1, 16, 4, row_above, ((4, 0), (0, 5))),
-        (0, 0, 5, row_below, ((5, 0), (0, 4))),
+        (1, 16, 4, above, ((4, 0), (0, 5))),
+        (0, 0, 5, below, ((5, 0), (0, 4))),
     ):
 
         @pl.when(J == end * last_j)
         def _():
+            swap = ((2, pole), (pole, 2))
+            ends = {
+                4: move_groups(from_left(mirror_ends[0], I == last_i), swap, masks),
+                0: move_groups(from_right(mirror_ends[1], I == 0), swap, masks),
+            }
             for x in range(5):
                 value = move_groups(ring[x], ring_pairs, masks)
                 value = value + move_groups(mirror[0], ((4 - x, pole),), masks)
                 value = value + move_groups(mirror[1], ((4 - x, 2),), masks)
                 value = value + move_groups(polar[0], ((x if end == 1 else 4 - x, 1),), masks)
                 value = value + move_groups(polar[1], ((4 - x if end == 1 else x, 3),), masks)
+                if x in ends:
+                    value = value + ends[x]
                 add(x, y, value)
 
             def extra(x):
@@ -553,22 +603,26 @@
         @pl.when(I == side * last_i)
         def _():
             group = 1 if side == 1 else 3
-            for end in range(2):
-                pole = 4 if end == 1 else 5
-                forward = side == end
-                for y in range(17):
-                    point = y if forward else 16 - y
-                    j, x = min(point // 4, 3), point - 4 * min(point // 4, 3)
-
-                    def place(y=y, j=j, x=x):
-                        add(4 * side, y, move_groups(slots[end, j], ((x, pole),), masks))
-
-                    if y == 0:
-                        pl.when(J != 0)(place)
-                    elif y == 16:
-                        pl.when(J != last_j)(place)
-                    else:
-                        place()
+            for y in range(17):
+
+                def place(y=y):
+                    value = None
+                    for end in range(2):
+                        pole = 4 if end == 1 else 5
+                        point = y if side == end else 16 - y
+                        parts = [move_groups(slots[end, j], ((point - 4 * j, pole),), masks) for j in range(4) if 0 <= point - 4 * j <= 4]
+                        if y in (0, 16):
+                            parts.append(move_groups(beyond[end, y // 16], ((group, pole),), masks))
+                        for part in parts:
+                            value = part if value is None else value + part
+                    add(4 * side, y, value)
+
+                if y == 0:
+                    pl.when(J != 0)(place)
+                elif y == 16:
+                    pl.when(J != last_j)(place)
+                else:
+                    place()
 
 
 def output_phase(load_tile, ins, outs):
@@ -610,8 +664,8 @@
 
 
 def local_kernel(n_xi, n_eta, *refs):
-    sources, keep, z, bufs = refs[:20], refs[20:26], refs[26], refs[27:35]
-    ins, (wide, narrow), outgoing, (fetch, send, recv) = refs[35:55], refs[55:57], refs[57:61], refs[61:]
+    sources, keep, z, bufs = refs[:20], refs[20:26], refs[26], refs[27:38]
+    ins, (wide, narrow), outgoing, (fetch, send, recv) = refs[38:58], refs[58:60], refs[60:63], refs[63:]
     fetches = [pltpu.make_async_copy(sources[n], ins[n], fetch.at[n]) for n in FETCH]
     for item in fetches:
         item.start()
@@ -633,8 +687,8 @@
 
 
 def output_kernel(n_xi, n_eta, *refs):
-    z, bufs, kept, halves = refs[0], refs[1:9], refs[9:12], refs[12:15]
-    copies_out, outs, (work, sem) = refs[15:18], refs[18:24], refs[24:]
+    z, bufs, kept, halves = refs[0], refs[1:12], refs[12:15], refs[15:18]
+    copies_out, outs, (work, sem) = refs[18:21], refs[21:27], refs[27:]
     writes = [pltpu.make_async_copy(kept[n], copies_out[n], sem.at[n]) for n in range(3)]
     for item in writes:
         item.start()
@@ -672,7 +726,7 @@
             + (shape(5, ROWS, 8, LANES),)
             + tuple(shape(*dims) for dims in EXCHANGE_SHAPES),
             in_specs=[hbm] * 20,
-            out_specs=[vmem] * 15,
+            out_specs=[vmem] * 18,
             scratch_shapes=[pltpu.VMEM(a.shape, F32) for a in ins]
             + [
                 pltpu.VMEM((PAD, 384), F32),
@@ -692,7 +746,7 @@
         outs = pl.pallas_call(
             functools.partial(output_kernel, n_xi, n_eta),
             out_shape=(big, thin, small) + (big, big, thin, thin, small, small),
-            in_specs=[vmem] * 15,
+            in_specs=[vmem] * 18,
             out_specs=[hbm] * 3 + [vmem] * 6,
             scratch_shapes=[pltpu.VMEM((5, ROWS, 8, LANES), F32), pltpu.SemaphoreType.DMA((3,))],
             compiler_params=pltpu.CompilerParams(vmem_limit_bytes=32 * 1024 * 1024),

time: 35.7 us -> 32.5 us (0.910)
  the two profiles are of different devices: /device:TPU:2 before, /device:TPU:16 now
where the time goes in v4:
time: 32.5 us; the launch traced here: 32.4 us
  Pallas kernels  31.7 us (98%)
  between operations  0.66 us (2%)
    pallas_call x1, Pallas kernels, step(): pl.pallas_call(functools.partial(local_kernel, n_xi, n_eta), out_shape=(b...  30.1 us
    pallas_call x1, Pallas kernels, step(): pl.pallas_call(functools.partial(output_kernel, n_xi, n_eta), out_shape=(...  1.58 us

profile of v4, /device:TPU:16, one launch (start us, length us, event | category | flops | bytes accessed | tf_op | source)
XLA Modules:
  0.0 32.4 jit_solution(13389090200263891736)
XLA Ops:
  0.6 30.1 %shard_map.259 = (f32[17,3,270]{2,1,0:T(4,128)S(1)}, f32[17,270]{1,0:T(8,128)S(1)}, f32[17,3,150]{2,1,0:T(4,128)S(1)}, f32[17,3,270]{2,1,0:T(4,128)S(1)}, f32[17...) custom-call(f32[17,3,270]{2,1,0:T(4,128)} %bitcast.17, ...), custom_call_target="tpu_custom_call" | custom-call | tf_op jit(solution)/shard_map/pallas_call | solution.py:723
  30.8 1.6 %shard_map.260 = (f32[17,3,270]{2,1,0:T(4,128)}, f32[17,270]{1,0:T(8,128)}, f32[17,3,150]{2,1,0:T(4,128)}, f32[17,3,270]{2,1,0:T(4,128)}, f32[17,3,270]{2,1,0:T(...) custom-call(f32[5,17,8,128]{3,2,1,0:T(8,128)S(1)} %get-tuple-element.36.refs_0_, ...), custom_call_target="tpu_custom_call" | custom-call | tf_op jit(solution)/shard_map/pallas_call | solution.py:746

commit v5 on v4

--- a/solution.py
+++ b/solution.py
@@ -268,7 +268,7 @@
 def exchange_phase(n_xi, n_eta, z, bufs, sems, before_send):
     col_left, col_right, row_below, row_above, diagonal, mirror, mirror_ends, slots, beyond, polar, polar_extra = bufs[:11]
     out_sides, out_mirror, out_polar = bufs[11:]
-    send, recv = sems
+    send, recv, ready = sems
     I, J = lax.axis_index("xi"), lax.axis_index("eta")
     last_i, last_j = n_xi - 1, n_eta - 1
     half = n_xi // 2
@@ -305,48 +305,6 @@
             action()
         else:
             pl.when(condition)(action)
-
-    barrier = pltpu.get_barrier_semaphore()
-
-    def greet(i, j):
-        pl.semaphore_signal(barrier, inc=1, device_id=(i, j), device_id_type=MESH)
-
-    @pl.when(at_edge)
-    def _():
-        greet(last_i - I, J)
-        pl.when(no_turn_after)(lambda: greet(before_mirror, J))
-        pl.when(no_turn_before)(lambda: greet(after_mirror, J))
-        pl.when(I != last_i)(lambda: greet(last_i, j_right))
-        pl.when(I != 0)(lambda: greet(0, j_left))
-
-        @pl.when(has_extra)
-        def _():
-            @pl.when(I % last_i != 0)
-            def _():
-                greet(last_i, j_right + lean)
-                greet(0, j_left - lean)
-
-    @pl.when(at_side)
-    def _():
-        for q in range(4):
-            guarded(J != last_j if q == 3 else None, functools.partial(greet, i_top(q), last_j))
-            guarded(J != 0 if q == 0 else None, functools.partial(greet, i_bottom(q), 0))
-        for q, exists in ((-1, J != 0), (4, J != last_j)):
-            guarded(exists, functools.partial(greet, i_top(q), last_j))
-            guarded(exists, functools.partial(greet, i_bottom(q), 0))
-
-    for i in (left, I, right):
-        for j in (down, J, up):
-            if not (i is I and j is J):
-                greet(i, j)
-
-    before_send()
-
-    turned_after = (I + 1) // half - I // half
-    turned_before = (I + n_xi) // half - (I + n_xi - 1) // half
-    edge_partners = 5 - turned_after - turned_before - far - near + 2 * (extra - far - near)
-    side_partners = 12 - 3 * top - 3 * bottom
-    pl.semaphore_wait(barrier, 8 + (top + bottom) * edge_partners + (far + near) * side_partners)
 
     base = [
         copy(z.at[0, 16], diagonal.at[1], SEND_DIAGONALS, RECV_DIAGONALS + 1, (left, up)),
@@ -391,20 +349,66 @@
             copies.append((copy(src, dst, s + 1, RECV_EXTRA + 1 - far, (i_bottom(q), 0)), exists))
         return copies
 
+    turned_after = (I + 1) // half - I // half
+    turned_before = (I + n_xi) // half - (I + n_xi - 1) // half
+    q_far = top * (I % 4) + (1 - top) * (3 - I % 4)
+    q_near = top * (3 - I % 4) + (1 - top) * (I % 4)
+    edge, side = top + bottom, far + near
+    mains, extras = main_copies(), extra_copies()
+    edges = [
+        (1, (left, J), 1, base[6:7]),
+        (1, (right, J), 0, base[7:8]),
+        (1, (I, up), 3, base[4:5]),
+        (1, (I, down), 2, base[5:6]),
+        (1, (left, up), 7, base[0:1]),
+        (1, (right, up), 6, base[1:2]),
+        (1, (left, down), 5, base[2:3]),
+        (1, (right, down), 4, base[3:4]),
+        (edge, (last_i - I, J), 8, [to_mirror]),
+        (edge * (1 - turned_after), (before_mirror, J), 9, [to_before]),
+        (edge * (1 - turned_before), (after_mirror, J), 10, [to_after]),
+        (edge * (1 - far), (last_i, j_right), 15 + 4 * top + q_far, [to_far]),
+        (edge * (1 - near), (0, j_left), 15 + 4 * top + q_near, [to_near]),
+        (edge * (extra - side), (last_i, j_right + lean), 23 + 2 * top + beyond_far, [past_far]),
+        (edge * (extra - side), (0, j_left - lean), 23 + 2 * top + beyond_near, [past_near]),
+    ]
+    for end in range(2):
+        for q in range(4):
+            partner = (i_top(q), last_j) if end == 1 else (i_bottom(q), 0)
+            own = top if (end, q) == (1, 3) else bottom if (end, q) == (0, 0) else 0
+            edges.append((side * (1 - own), partner, 12 - far, [mains[2 * q + 1 - end][0]]))
+    for end in range(2):
+        for n, q in ((0, -1), (1, 4)):
+            partner = (i_top(q), last_j) if end == 1 else (i_bottom(q), 0)
+            edges.append((side * (1 - (bottom, top)[n]), partner, 14 - far, [extras[2 * n + 1 - end][0]]))
+
+    def depth(i):
+        return (i // 2) % 8
+
+    def key(i, j):
+        x, y = j % 8, 4 * (j // 8) + i // 16
+        return (12 * depth(i) + x * (8 - x) + y * (8 - y)) * (n_xi * n_eta) + i * n_eta + j
+
+    many = 256 * n_xi * n_eta
+    mine = key(I, J)
+    earlier = [exists * ((mine - key(*partner) + many) // many) for exists, partner, _, _ in edges]
+    later = [edges[n][0] - earlier[n] for n in range(len(edges))]
+
+    barrier = pltpu.get_barrier_semaphore()
+
+    def tell(semaphore, partner):
+        pl.semaphore_signal(semaphore, inc=1, device_id=partner, device_id_type=MESH)
+
+    near_first = [*range(8, 27), *range(8)]
+    for n in near_first:
+        pl.when(later[n] == 1)(functools.partial(tell, barrier, edges[n][1]))
+
+    before_send()
+
     masks = group_masks((8, LANES))
 
     @pl.when(at_edge)
     def _():
-        pl.when(no_turn_after)(to_before.start)
-        pl.when(no_turn_before)(to_after.start)
-
-        @pl.when(has_extra)
-        def _():
-            @pl.when(I % last_i != 0)
-            def _():
-                past_far.start()
-                past_near.start()
-
         for end in range(2):
 
             @pl.when(J == end * last_j)
@@ -415,23 +419,29 @@
                 out_mirror[0] = pack_group(rows, 2, masks)
                 out_mirror[1] = pack_group(rows, 4 if end == 1 else 5, masks)
 
-        pl.when(I != last_i)(to_far.start)
-        pl.when(I != 0)(to_near.start)
-        to_mirror.start()
-
     @pl.when(at_side)
     def _():
-        for item, condition in extra_copies():
-            guarded(condition, item.start)
         for q in range(4):
             rows = [z[4 * far, 4 * q + i] for i in range(5)]
             out_polar[1, q] = pack_group(rows, 4, masks)
             out_polar[0, q] = pack_group(rows, 5, masks)
-        for item, condition in main_copies():
-            guarded(condition, item.start)
-
-    for item in base:
-        item.start()
+
+    present = sum(earlier)
+    pl.when(present != 0)(lambda: pl.semaphore_wait(barrier, present))
+
+    for n in near_first:
+        pl.when(earlier[n] == 1)(functools.partial(lambda n: tell(ready.at[edges[n][2]], edges[n][1]), n))
+
+    def start(n):
+        for item in edges[n][3]:
+            item.start()
+
+    def start_when_ready(n):
+        pl.semaphore_wait(ready.at[n], 1)
+        start(n)
+
+    for n in near_first:
+        pl.when(earlier[n] == 1)(functools.partial(start, n))
 
     @pl.when(at_edge)
     def _():
@@ -444,6 +454,11 @@
     def _():
         pl.when(J == last_j)(lambda: polar.__setitem__(1 - far, out_polar[1, 3]))
         pl.when(J == 0)(lambda: polar.__setitem__(1 - far, out_polar[0, 0]))
+
+    for level in range(3):
+        for n in (1, 2, 3, 5, 7, *range(8, 27), 0, 4, 6):
+            at_level = (depth(edges[n][1][0]) // 3 - level) * (depth(edges[n][1][0]) // 3 - level)
+            pl.when(later[n] * 10 - at_level == 10)(functools.partial(start_when_ready, n))
 
     for item in base:
         item.wait_recv()
@@ -665,12 +680,12 @@
 
 def local_kernel(n_xi, n_eta, *refs):
     sources, keep, z, bufs = refs[:20], refs[20:26], refs[26], refs[27:38]
-    ins, (wide, narrow), outgoing, (fetch, send, recv) = refs[38:58], refs[58:60], refs[60:63], refs[63:]
+    ins, (wide, narrow), outgoing, (fetch, send, recv, ready) = refs[38:58], refs[58:60], refs[60:63], refs[63:]
     fetches = [pltpu.make_async_copy(sources[n], ins[n], fetch.at[n]) for n in FETCH]
     for item in fetches:
         item.start()
 
-    def ready(steps):
+    def landed(steps):
         for n in steps:
             fetches[n].wait()
 
@@ -681,9 +696,9 @@
     def work():
         for t in (6, 7):
             store_tile(t, jnp.zeros((5, ROWS, LANES), F32))
-        local_phase(ins, keep, store_tile, (wide, narrow), ready)
-
-    exchange_phase(n_xi, n_eta, z, bufs + outgoing, (send, recv), work)
+        local_phase(ins, keep, store_tile, (wide, narrow), landed)
+
+    exchange_phase(n_xi, n_eta, z, bufs + outgoing, (send, recv, ready), work)
 
 
 def output_kernel(n_xi, n_eta, *refs):
@@ -737,6 +752,7 @@
                 pltpu.SemaphoreType.DMA((20,)),
                 pltpu.SemaphoreType.DMA((SENDS,)),
                 pltpu.SemaphoreType.DMA((RECEIVES,)),
+                pltpu.SemaphoreType.REGULAR((27,)),
             ],
             compiler_params=pltpu.CompilerParams(
                 collective_id=0, has_side_effects=True, vmem_limit_bytes=32 * 1024 * 1024

time: 32.5 us -> 33.5 us (1.031)
  Pallas kernels: 31.7 us -> 32.7 us
    pallas_call x1, Pallas kernels: 30.1 us -> 31.1 us  [step(): pl.pallas_call(functools.partial(local_kernel, n_xi, n_eta), out_shape=(b...]
where the time goes in v5:
time: 33.5 us; the launch traced here: 33.3 us
  Pallas kernels  32.7 us (98%)
  between operations  0.66 us (2%)
    pallas_call x1, Pallas kernels, step(): pl.pallas_call(functools.partial(local_kernel, n_xi, n_eta), out_shape=(b...  31.1 us
    pallas_call x1, Pallas kernels, step(): pl.pallas_call(functools.partial(output_kernel, n_xi, n_eta), out_shape=(...  1.58 us

profile of v5, /device:TPU:16, one launch (start us, length us, event | category | flops | bytes accessed | tf_op | source)
XLA Modules:
  0.0 33.3 jit_solution(3869898389771249045)
XLA Ops:
  0.6 31.1 %shard_map.259 = (f32[17,3,270]{2,1,0:T(4,128)S(1)}, f32[17,270]{1,0:T(8,128)S(1)}, f32[17,3,150]{2,1,0:T(4,128)S(1)}, f32[17,3,270]{2,1,0:T(4,128)S(1)}, f32[17...) custom-call(f32[17,3,270]{2,1,0:T(4,128)} %bitcast.17, ...), custom_call_target="tpu_custom_call" | custom-call | tf_op jit(solution)/shard_map/pallas_call | solution.py:738
  31.7 1.6 %shard_map.260 = (f32[17,3,270]{2,1,0:T(4,128)}, f32[17,270]{1,0:T(8,128)}, f32[17,3,150]{2,1,0:T(4,128)}, f32[17,3,270]{2,1,0:T(4,128)}, f32[17,3,270]{2,1,0:T(...) custom-call(f32[5,17,8,128]{3,2,1,0:T(8,128)S(1)} %get-tuple-element.36.refs_0_, ...), custom_call_target="tpu_custom_call" | custom-call | tf_op jit(solution)/shard_map/pallas_call | solution.py:762

commit v6 on v4

--- a/solution.py
+++ b/solution.py
@@ -342,12 +342,6 @@
 
     before_send()
 
-    turned_after = (I + 1) // half - I // half
-    turned_before = (I + n_xi) // half - (I + n_xi - 1) // half
-    edge_partners = 5 - turned_after - turned_before - far - near + 2 * (extra - far - near)
-    side_partners = 12 - 3 * top - 3 * bottom
-    pl.semaphore_wait(barrier, 8 + (top + bottom) * edge_partners + (far + near) * side_partners)
-
     base = [
         copy(z.at[0, 16], diagonal.at[1], SEND_DIAGONALS, RECV_DIAGONALS + 1, (left, up)),
         copy(z.at[4, 16], diagonal.at[0], SEND_DIAGONALS + 1, RECV_DIAGONALS, (right, up)),
@@ -395,16 +389,6 @@
 
     @pl.when(at_edge)
     def _():
-        pl.when(no_turn_after)(to_before.start)
-        pl.when(no_turn_before)(to_after.start)
-
-        @pl.when(has_extra)
-        def _():
-            @pl.when(I % last_i != 0)
-            def _():
-                past_far.start()
-                past_near.start()
-
         for end in range(2):
 
             @pl.when(J == end * last_j)
@@ -415,14 +399,43 @@
                 out_mirror[0] = pack_group(rows, 2, masks)
                 out_mirror[1] = pack_group(rows, 4 if end == 1 else 5, masks)
 
-        pl.when(I != last_i)(to_far.start)
-        pl.when(I != 0)(to_near.start)
-        to_mirror.start()
+    turned_after = (I + 1) // half - I // half
+    turned_before = (I + n_xi) // half - (I + n_xi - 1) // half
+    edge_partners = 5 - turned_after - turned_before - far - near + 2 * (extra - far - near)
+    side_partners = 12 - 3 * top - 3 * bottom
+    pl.semaphore_wait(barrier, 8 + (top + bottom) * edge_partners + (far + near) * side_partners)
 
     @pl.when(at_side)
     def _():
         for item, condition in extra_copies():
             guarded(condition, item.start)
+
+    @pl.when(at_edge)
+    def _():
+        pl.when(I != 0)(to_near.start)
+        pl.when(I != last_i)(to_far.start)
+
+    for item in base[:4]:
+        item.start()
+
+    @pl.when(at_edge)
+    def _():
+        pl.when(no_turn_after)(to_before.start)
+        pl.when(no_turn_before)(to_after.start)
+        to_mirror.start()
+
+        @pl.when(has_extra)
+        def _():
+            @pl.when(I % last_i != 0)
+            def _():
+                past_far.start()
+                past_near.start()
+
+    for item in base[4:6]:
+        item.start()
+
+    @pl.when(at_side)
+    def _():
         for q in range(4):
             rows = [z[4 * far, 4 * q + i] for i in range(5)]
             out_polar[1, q] = pack_group(rows, 4, masks)
@@ -430,7 +443,7 @@
         for item, condition in main_copies():
             guarded(condition, item.start)
 
-    for item in base:
+    for item in base[6:]:
         item.start()
 
     @pl.when(at_edge)
@@ -444,6 +457,29 @@
     def _():
         pl.when(J == last_j)(lambda: polar.__setitem__(1 - far, out_polar[1, 3]))
         pl.when(J == 0)(lambda: polar.__setitem__(1 - far, out_polar[0, 0]))
+
+    for item in base:
+        item.wait_send()
+
+    @pl.when(at_edge)
+    def _():
+        to_mirror.wait_send()
+        pl.when(no_turn_after)(to_before.wait_send)
+        pl.when(no_turn_before)(to_after.wait_send)
+        pl.when(I != last_i)(to_far.wait_send)
+        pl.when(I != 0)(to_near.wait_send)
+
+        @pl.when(has_extra)
+        def _():
+            @pl.when(I % last_i != 0)
+            def _():
+                past_far.wait_send()
+                past_near.wait_send()
+
+    @pl.when(at_side)
+    def _():
+        for item, condition in main_copies() + extra_copies():
+            guarded(condition, item.wait_send)
 
     for item in base:
         item.wait_recv()
@@ -477,29 +513,6 @@
             for n, exists in ((0, J != 0), (1, J != last_j)):
                 arrival = copy(z.at[0, 0], beyond.at[end, n], SEND_BEYOND, RECV_BEYOND + 2 * end + n, (left, J))
                 pl.when(exists)(arrival.wait_recv)
-
-    for item in base:
-        item.wait_send()
-
-    @pl.when(at_edge)
-    def _():
-        to_mirror.wait_send()
-        pl.when(no_turn_after)(to_before.wait_send)
-        pl.when(no_turn_before)(to_after.wait_send)
-        pl.when(I != last_i)(to_far.wait_send)
-        pl.when(I != 0)(to_near.wait_send)
-
-        @pl.when(has_extra)
-        def _():
-            @pl.when(I % last_i != 0)
-            def _():
-                past_far.wait_send()
-                past_near.wait_send()
-
-    @pl.when(at_side)
-    def _():
-        for item, condition in main_copies() + extra_copies():
-            guarded(condition, item.wait_send)
 
 
 EXCHANGE_SHAPES = (
@@ -523,7 +536,6 @@
     I, J = lax.axis_index("xi"), lax.axis_index("eta")
     last_i, last_j = n_xi - 1, n_eta - 1
     masks = group_masks((8, LANES))
-    big_masks = group_masks((17, 8, LANES))
 
     def add(x, y, values):
         work[x, y] += values
@@ -551,11 +563,11 @@
 
     @pl.when(I == 0)
     def _():
-        work[0] += move_groups(col_left[...], FROM_LEFT, big_masks)
+        work[0] += move_groups(col_left[...], FROM_LEFT, masks)
 
     @pl.when(I == last_i)
     def _():
-        work[4] += move_groups(col_right[...], FROM_RIGHT, big_masks)
+        work[4] += move_groups(col_right[...], FROM_RIGHT, masks)
 
     @pl.when(J != last_j)
     def _():
@@ -625,7 +637,7 @@
                     place()
 
 
-def output_phase(load_tile, ins, outs):
+def output_phase(load_tile, ins, outs, leave):
     mv_half, cr_half, nv_half = ins
     mv_new, ma_new, cr_new, ca_new, nv_new, na_new = outs
     lane = lane_index((1, ROWS, LANES))
@@ -647,17 +659,21 @@
             result = moved if result is None else jnp.where(lanes_out >= count * x, moved, result)
         return result
 
-    for i in range(3):
-        new = (force if i == 2 else load_tile(i)) / mass
-        outer = gather(new, 0, 54, 384)[:, :270]
-        ma_new[:, i, :] = outer
-        mv_new[:, i, :] = mv_half[:, i, :] + HALF_STEP * outer
-        inner = gather(new, 54, 30, 256)[:, :150]
-        na_new[:, i, :] = inner
-        nv_new[:, i, :] = nv_half[:, i, :] + HALF_STEP * inner
     outer = gather(accel, 0, 54, 384)[:, :270]
     ca_new[...] = outer
     cr_new[...] = cr_half[...] + HALF_STEP * outer
+    leave((2, 3))
+    accels = [(force if i == 2 else load_tile(i)) / mass for i in range(3)]
+    for i in range(3):
+        outer = gather(accels[i], 0, 54, 384)[:, :270]
+        ma_new[:, i, :] = outer
+        mv_new[:, i, :] = mv_half[:, i, :] + HALF_STEP * outer
+    leave((0, 1))
+    for i in range(3):
+        inner = gather(accels[i], 54, 30, 256)[:, :150]
+        na_new[:, i, :] = inner
+        nv_new[:, i, :] = nv_half[:, i, :] + HALF_STEP * inner
+    leave((4, 5))
 
 
 FETCH = (0, 1, 2, 12, 13, 14, 18, 19, 3, 15, 4, 16, 5, 17, 6, 7, 8, 9, 10, 11)
@@ -667,9 +683,6 @@
     sources, keep, z, bufs = refs[:20], refs[20:26], refs[26], refs[27:38]
     ins, (wide, narrow), outgoing, (fetch, send, recv) = refs[38:58], refs[58:60], refs[60:63], refs[63:]
     fetches = [pltpu.make_async_copy(sources[n], ins[n], fetch.at[n]) for n in FETCH]
-    for item in fetches:
-        item.start()
-
     def ready(steps):
         for n in steps:
             fetches[n].wait()
@@ -679,6 +692,8 @@
             z[x, :, t, :] = values[x, :ROWS]
 
     def work():
+        for item in fetches:
+            item.start()
         for t in (6, 7):
             store_tile(t, jnp.zeros((5, ROWS, LANES), F32))
         local_phase(ins, keep, store_tile, (wide, narrow), ready)
@@ -688,17 +703,21 @@
 
 def output_kernel(n_xi, n_eta, *refs):
     z, bufs, kept, halves = refs[0], refs[1:12], refs[12:15], refs[15:18]
-    copies_out, outs, (work, sem) = refs[18:21], refs[21:27], refs[27:]
-    writes = [pltpu.make_async_copy(kept[n], copies_out[n], sem.at[n]) for n in range(3)]
-    for item in writes:
-        item.start()
+    out_refs, outs, (work, sem) = refs[18:27], refs[27:33], refs[33:]
+    writes = [pltpu.make_async_copy(src, dst, sem.at[n]) for n, (src, dst) in enumerate(zip(kept + outs, out_refs))]
+
+    def leave(numbers):
+        for n in numbers:
+            writes[3 + n].start()
+
+    leave((-3, -2, -1))
     work[...] = z[...]
     total_phase(n_xi, n_eta, work, bufs)
 
     def load_tile(t):
         return jnp.stack([work[x, :, t, :] for x in range(5)])
 
-    output_phase(load_tile, halves, outs)
+    output_phase(load_tile, halves, outs, leave)
     for item in writes:
         item.wait()
 
@@ -747,8 +766,9 @@
             functools.partial(output_kernel, n_xi, n_eta),
             out_shape=(big, thin, small) + (big, big, thin, thin, small, small),
             in_specs=[vmem] * 18,
-            out_specs=[hbm] * 3 + [vmem] * 6,
-            scratch_shapes=[pltpu.VMEM((5, ROWS, 8, LANES), F32), pltpu.SemaphoreType.DMA((3,))],
+            out_specs=[hbm] * 9,
+            scratch_shapes=[pltpu.VMEM(a.shape, F32) for a in (big, big, thin, thin, small, small)]
+            + [pltpu.VMEM((5, ROWS, 8, LANES), F32), pltpu.SemaphoreType.DMA((9,))],
             compiler_params=pltpu.CompilerParams(vmem_limit_bytes=32 * 1024 * 1024),
         )(z, *bufs, *kept, *halves)
         md_new, cp_new, nd_new, mv_new, ma_new, cr_new, ca_new, nv_new, na_new = [

time: 32.5 us -> 32.6 us (level)
  no operation moved by 1% of the time
where the time goes in v6:
time: 32.6 us; the launch traced here: 32.4 us
  Pallas kernels  31.7 us (97%)
  between operations  0.66 us (2%)
    pallas_call x1, Pallas kernels, step(): pl.pallas_call(functools.partial(local_kernel, n_xi, n_eta), out_shape=(b...  30.2 us
    pallas_call x1, Pallas kernels, step(): pl.pallas_call(functools.partial(output_kernel, n_xi, n_eta), out_shape=(...  1.54 us

profile of v6, /device:TPU:16, one launch (start us, length us, event | category | flops | bytes accessed | tf_op | source)
XLA Modules:
  0.0 32.4 jit_solution(12939057946625698885)
XLA Ops:
  0.6 30.2 %shard_map.259 = (f32[17,3,270]{2,1,0:T(4,128)S(1)}, f32[17,270]{1,0:T(8,128)S(1)}, f32[17,3,150]{2,1,0:T(4,128)S(1)}, f32[17,3,270]{2,1,0:T(4,128)S(1)}, f32[17...) custom-call(f32[17,3,270]{2,1,0:T(4,128)} %bitcast.17, ...), custom_call_target="tpu_custom_call" | custom-call | tf_op jit(solution)/shard_map/pallas_call | solution.py:742
  30.8 1.5 %shard_map.260 = (f32[17,3,270]{2,1,0:T(4,128)}, f32[17,270]{1,0:T(8,128)}, f32[17,3,150]{2,1,0:T(4,128)}, f32[17,3,270]{2,1,0:T(4,128)}, f32[17,3,270]{2,1,0:T(...) custom-call(f32[5,17,8,128]{3,2,1,0:T(8,128)S(1)} %get-tuple-element.36.refs_0_, ...), custom_call_target="tpu_custom_call" | custom-call | tf_op jit(solution)/shard_map/pallas_call | solution.py:765

commit v7 on v6

--- a/solution.py
+++ b/solution.py
@@ -484,6 +484,22 @@
     for item in base:
         item.wait_recv()
 
+    @pl.when(I != 0)
+    def _():
+        z[0] += col_left[...]
+
+    @pl.when(I != last_i)
+    def _():
+        z[4] += col_right[...]
+
+    @pl.when(I == 0)
+    def _():
+        z[0] += move_groups(col_left[...], FROM_LEFT, masks)
+
+    @pl.when(I == last_i)
+    def _():
+        z[4] += move_groups(col_right[...], FROM_RIGHT, masks)
+
     @pl.when(at_edge)
     def _():
         to_mirror.wait_recv()
@@ -552,22 +568,6 @@
 
     below = completed(row_below, 0, 1)
     above = completed(row_above, 2, 3)
-
-    @pl.when(I != 0)
-    def _():
-        work[0] += col_left[...]
-
-    @pl.when(I != last_i)
-    def _():
-        work[4] += col_right[...]
-
-    @pl.when(I == 0)
-    def _():
-        work[0] += move_groups(col_left[...], FROM_LEFT, masks)
-
-    @pl.when(I == last_i)
-    def _():
-        work[4] += move_groups(col_right[...], FROM_RIGHT, masks)
 
     @pl.when(J != last_j)
     def _():

time: 32.6 us -> 32.5 us (level)
  no operation moved by 1% of the time
where the time goes in v7:
time: 32.5 us; the launch traced here: 32.4 us
  Pallas kernels  31.7 us (98%)
  between operations  0.66 us (2%)
    pallas_call x1, Pallas kernels, step(): pl.pallas_call(functools.partial(local_kernel, n_xi, n_eta), out_shape=(b...  30.2 us
    pallas_call x1, Pallas kernels, step(): pl.pallas_call(functools.partial(output_kernel, n_xi, n_eta), out_shape=(...  1.51 us

profile of v7, /device:TPU:16, one launch (start us, length us, event | category | flops | bytes accessed | tf_op | source)
XLA Modules:
  0.0 32.4 jit_solution(3123755210550778562)
XLA Ops:
  0.6 30.2 %shard_map.259 = (f32[17,3,270]{2,1,0:T(4,128)S(1)}, f32[17,270]{1,0:T(8,128)S(1)}, f32[17,3,150]{2,1,0:T(4,128)S(1)}, f32[17,3,270]{2,1,0:T(4,128)S(1)}, f32[17...) custom-call(f32[17,3,270]{2,1,0:T(4,128)} %bitcast.17, ...), custom_call_target="tpu_custom_call" | custom-call | tf_op jit(solution)/shard_map/pallas_call | solution.py:742
  30.8 1.5 %shard_map.260 = (f32[17,3,270]{2,1,0:T(4,128)}, f32[17,270]{1,0:T(8,128)}, f32[17,3,150]{2,1,0:T(4,128)}, f32[17,3,270]{2,1,0:T(4,128)}, f32[17,3,270]{2,1,0:T(...) custom-call(f32[5,17,8,128]{3,2,1,0:T(8,128)S(1)} %get-tuple-element.36.refs_0_, ...), custom_call_target="tpu_custom_call" | custom-call | tf_op jit(solution)/shard_map/pallas_call | solution.py:765
